TPU v7x, 128 devices: a whole 4x4x4 slice. The times are simulated.
128 devices in a mesh: group: 8 (over y, core), tp: 16 (over x, z).
Axes of the slice: x: 4, y: 4, z: 4, core: 2. Of those that a mesh axis runs over, the one named last changes fastest.
Arguments:
- residual: bfloat16 [768, 4096], P('group', 'tp'), may hold values from -18 to 18
- tree_qkv: bfloat16 [3, 768, 4096], P(None, 'group', 'tp'), may hold values from -12.5 to 12.5
- kv_pool: bfloat16 [2, 256, 128, 4096], P(None, 'group', None, 'tp'), may hold values from -12.5 to 12.5
- page_table: int32 [16, 28], replicated, may hold values from 0 to 31, as said below
- cache_len: int32 [16], replicated, may hold values from 1 to 3584, as said below
- tree_parent: int32 [16, 48], replicated, may hold values from 0 to 46, as said below
- accepted_nodes: int32 [16, 4], P('group'), may hold values from 0 to 47
- out_weight: bfloat16 [4096, 4096], P('tp'), may hold values from -0.125 to 0.125
- norm_gain: float32 [4096], P('tp'), may hold values from 0.5 to 1.5
- draft_weight: bfloat16 [3, 4096, 4096], P(None, None, 'tp'), may hold values from -0.09375 to 0.09375
- vocab_weight: bfloat16 [26624, 4096], P('tp'), may hold values from -1.75 to 1.75
- target_ids: int32 [4, 768], P(None, 'group'), may hold values from 0 to 26623
Outputs:
- log_probs: float32 [4, 768], P(None, 'group')
- accepted_kv: bfloat16 [2, 64, 4096], P(None, 'group', 'tp')
Inputs may be any that keep to these rules, and one draw needn't show every extreme that they name: `cache_len`: request 2 g is group g's short request and request 2 g + 1 its long one; a short request has at most 512 positions and some group's has exactly that many; a long request has 128 or more and some group's has exactly 3584. `page_table`: entries of request r of group g = r // 2 are slots of group g's pool, except the odd columns of a long request, which are slots of group g xor 1's pool. In each group's pool the short request's first 4 columns, its long request's even columns and the odd columns of group g xor 1's long request are distinct slots covering the pool; a short request's columns from 4 on repeat its first ones. `tree_parent`: node 0 is the root and its own parent; every other node's parent has a smaller index, and node 48 - 1's parent is node 46.
All inputs are finite; a program needn't handle non-finite values.
Results may differ from a plain program's by a relative error of at most 0.004.
Values may be sent and summed in bfloat16 or wider, within the bound.
A program may use at most 128 MiB of HBM per device.

v0:
```python
import math

import jax
import jax.numpy as jnp
from jax import lax
from jax.sharding import PartitionSpec as P

D = 4096
HEADS = 32
HD = 128
TREE = 48
SHORT_PAGES = 4
LONG_PAGES = 28


EPSILON = 1e-05


def from_partner(block, axis, apart):
    count = lax.axis_size(axis)
    route = []
    for low in range(count):
        high = low | 1 << apart
        if high != low and high < count:
            route += [(low, high), (high, low)]
    return lax.ppermute(block, axis, route)


def combined_all(array, axis, combine):
    everything = jax.tree.map(lambda part: lax.all_gather(part, axis), array)
    leading = jax.tree.map(lambda part: part[0], everything)

    def turn(k, so_far):
        return combine(so_far, jax.tree.map(lambda part: part[k], everything))

    return lax.fori_loop(1, lax.axis_size(axis), turn, leading)


def ancestry(parents):
    number = parents.shape[0]
    indices = jnp.arange(number, dtype=jnp.int32)
    linked = ((parents[:, None] == indices[None, :]) & (indices[:, None] > 0)).astype(jnp.float32)
    reached = jnp.minimum(jnp.eye(number, dtype=jnp.float32) + linked, 1.0)
    for sweep_index in range(max(1, number.bit_length())):
        reached = jnp.minimum(jnp.dot(reached, reached, precision=lax.Precision.HIGHEST), 1.0)
    depths = jnp.sum(reached, axis=1) - 1.0
    return (reached, depths)


def slope_values(first, number):
    ordinal = jnp.arange(number, dtype=jnp.float32) + jnp.asarray(first, jnp.float32) + 1.0
    return jnp.exp2(-8.0 * ordinal / HEADS)


def partial_attention(queries, key_rows, value_rows, allowed, query_pos, key_pos, slopes):
    scores = jnp.einsum("thd,lhd->htl", queries, key_rows, preferred_element_type=jnp.float32) * (
        1.0 / math.sqrt(HD)
    )
    scores = scores - slopes[:, None, None] * (query_pos[None, :, None] - key_pos[None, None, :])
    row_top = jnp.max(jnp.where(allowed[None], scores, -1e30), axis=2)
    weights = jnp.where(allowed[None], jnp.exp(scores - row_top[:, :, None]), 0.0)
    weight_sum = jnp.sum(weights, axis=2)
    weighted = jnp.einsum(
        "htl,lhd->thd", weights, value_rows.astype(jnp.float32), precision=lax.Precision.HIGHEST
    )
    return (row_top, weight_sum, weighted)


def join_parts(earlier, later):
    joined = jnp.maximum(earlier[0], later[0])
    factor_one = jnp.exp(earlier[0] - joined)
    factor_two = jnp.exp(later[0] - joined)
    weight_sum = earlier[1] * factor_one + later[1] * factor_two
    weighted = (
        earlier[2] * jnp.transpose(factor_one)[:, :, None]
        + later[2] * jnp.transpose(factor_two)[:, :, None]
    )
    return (joined, weight_sum, weighted)


def page_attention(gathered, columns, queries, query_pos, length, slopes, heads_dev):
    number = gathered.shape[1]
    page_rows = gathered.shape[2]
    flat_pages = gathered.reshape(2, number * page_rows, heads_dev, HD)
    key_pos = (
        (columns[:, None] * page_rows + jnp.arange(page_rows)[None, :])
        .reshape(-1)
        .astype(jnp.float32)
    )
    allowed = jnp.broadcast_to(key_pos[None, :] < length, (queries.shape[0], key_pos.shape[0]))
    return partial_attention(
        queries, flat_pages[0], flat_pages[1], allowed, query_pos, key_pos, slopes
    )


def merge_softmax(earlier, later):
    joined = jnp.maximum(earlier[0], later[0])
    return (
        joined,
        earlier[1] * jnp.exp(earlier[0] - joined) + later[1] * jnp.exp(later[0] - joined),
        earlier[2] + later[2],
    )


def shards(
    residual,
    tree_qkv,
    kv_pool,
    page_table,
    cache_len,
    tree_parent,
    accepted_nodes,
    out_weight,
    norm_gain,
    draft_weight,
    vocab_weight,
    target_ids,
):
    lane_count = lax.axis_size("tp")
    lane_index = lax.axis_index("tp")
    group_index = lax.axis_index("group")
    partner = jnp.bitwise_xor(group_index, 1)
    heads_dev = HEADS // lane_count
    width_dev = residual.shape[1]
    slopes = slope_values(lane_index * heads_dev, heads_dev)
    odd_columns = jnp.arange(1, LONG_PAGES, 2, dtype=jnp.int32)
    attn_rows = []
    for slot_index in range(2):
        request = group_index * 2 + slot_index
        tree_block = tree_qkv[:, slot_index * TREE : (slot_index + 1) * TREE].reshape(
            3, TREE, heads_dev, HD
        )
        reached, depths = ancestry(tree_parent[request])
        length = cache_len[request].astype(jnp.float32)
        query_pos = length + depths
        merged = partial_attention(
            tree_block[0], tree_block[1], tree_block[2], reached > 0.5, query_pos, query_pos, slopes
        )
        table_row = page_table[request]
        if slot_index == 0:
            own_columns = jnp.arange(SHORT_PAGES, dtype=jnp.int32)
            own_slots = table_row[:SHORT_PAGES]
        else:
            own_columns = jnp.arange(0, LONG_PAGES, 2, dtype=jnp.int32)
            own_slots = table_row[0::2]
        own_pages = jnp.take(kv_pool, own_slots, axis=1)
        merged = join_parts(
            merged,
            page_attention(
                own_pages, own_columns, tree_block[0], query_pos, length, slopes, heads_dev
            ),
        )
        if slot_index == 1:
            guest_req = partner * 2 + 1
            visitors = from_partner(tree_block[0], "group", 0)
            guest_len = cache_len[guest_req].astype(jnp.float32)
            guest_pos = guest_len + ancestry(tree_parent[guest_req])[1]
            held_pages = jnp.take(kv_pool, page_table[guest_req][1::2], axis=1)
            guest_part = page_attention(
                held_pages, odd_columns, visitors, guest_pos, guest_len, slopes, heads_dev
            )
            returned = from_partner((guest_part[0], guest_part[1], guest_part[2]), "group", 0)
            merged = join_parts(merged, returned)
        row_top, weight_sum, weighted = merged
        attn_rows.append(
            (weighted / jnp.transpose(weight_sum)[:, :, None])
            .reshape(TREE, width_dev)
            .astype(jnp.bfloat16)
        )
    attn = jnp.concatenate(attn_rows, 0)
    head_term = jnp.dot(attn, out_weight, preferred_element_type=jnp.float32)
    head_share = lax.psum_scatter(
        head_term.astype(jnp.bfloat16), "tp", scatter_dimension=1, tiled=True
    ).astype(jnp.float32)
    hidden = residual.astype(jnp.float32) + head_share
    row_sums, squares = lax.psum((jnp.sum(hidden, axis=1), jnp.sum(hidden * hidden, axis=1)), "tp")
    row_mean = (row_sums / D)[:, None]
    row_var = (squares / D)[:, None] - row_mean * row_mean
    normed = ((hidden - row_mean) * lax.rsqrt(row_var + EPSILON) * norm_gain).astype(jnp.bfloat16)
    normed_full = lax.all_gather(normed, "tp", axis=1, tiled=True)
    updates = jnp.einsum(
        "td,kdc->ktc", normed_full, draft_weight, preferred_element_type=jnp.float32
    )
    drafted = (normed.astype(jnp.float32)[None] + jax.nn.silu(updates)).astype(jnp.bfloat16)
    vocab_dev = vocab_weight.shape[0]
    base_logits = lax.dot_general(
        vocab_weight, normed_full, (((1,), (1,)), ((), ())), preferred_element_type=jnp.float32
    )
    draft_logits = jnp.einsum(
        "vc,ktc->vkt",
        vocab_weight,
        lax.all_gather(drafted, "tp", axis=2, tiled=True),
        preferred_element_type=jnp.float32,
    )
    logits = jnp.concatenate([base_logits[:, None, :], draft_logits], 1)
    local_top = jnp.max(logits, axis=0)
    local_total = jnp.sum(jnp.exp(logits - local_top[None]), axis=0)
    vocab_ids = lane_index * vocab_dev + jnp.arange(vocab_dev, dtype=jnp.int32)
    matches = vocab_ids[:, None, None] == target_ids[None]
    local_pick = jnp.sum(jnp.where(matches, logits, 0.0), axis=0)
    global_top, global_total, picked = combined_all(
        (local_top, local_total, local_pick), "tp", merge_softmax
    )
    log_probs = picked - (global_top + jnp.log(global_total))
    flat_index = (jnp.arange(2, dtype=jnp.int32)[:, None] * TREE + accepted_nodes).reshape(-1)
    accepted_kv = jnp.take(tree_qkv[1:3], flat_index, axis=1)
    return (log_probs, accepted_kv)


def solution(mesh):
    placed = (
        P("group", "tp"),
        P(None, "group", "tp"),
        P(None, "group", None, "tp"),
        P(),
        P(),
        P(),
        P("group", None),
        P("tp", None),
        P("tp"),
        P(None, None, "tp"),
        P("tp", None),
        P(None, "group"),
    )
    return jax.shard_map(
        shards,
        mesh=mesh,
        in_specs=placed,
        out_specs=(P(None, "group"), P(None, "group", "tp")),
        check_vma=False,
    )
```

profile of v0, /device:TPU:0, one launch (start us, length us, event | category | flops | bytes accessed | tf_op | source)
XLA Modules:
  0.0 353.4 jit_solution(13451830431486187444)
XLA Ops:
  7.2 1.0 fusion.128
  11.9 1.4 fusion.129
  15.4 2.8 gather_fusion
  23.0 4.1 %gather_fusion.3 = bf16[14,2,128,256]{3,2,1,0:T(8,128)(2,1)} fusion(bf16[2,32,128,256]{3,2,1,0:T(8,128)(2,1)} %param.18, s32[1024]{0:T(1024)S(1)} %pad_clamp_fusion.1), kind=kCustom, calls=%fused_computation.1.clone | custom fusion | bytes 3670072 | tf_op jit(solution)/shard_map/jit(_take)/gather | solution.py:158
  27.2 1.7 select_bitcast_fusion
  28.9 1.1 fusion.126
  33.6 4.1 %gather_fusion.2 = bf16[14,2,128,256]{3,2,1,0:T(8,128)(2,1)} fusion(bf16[2,32,128,256]{3,2,1,0:T(8,128)(2,1)} %param.18, s32[1024]{0:T(1024)S(1)} %pad_clamp_fusion.2), kind=kCustom, calls=%fused_computation.clone | custom fusion | bytes 3670072 | tf_op jit(solution)/shard_map/jit(_take)/gather | solution.py:146
  37.7 1.7 select_bitcast_fusion.1
  39.4 1.4 fusion.125
  40.8 2.9 squeeze.97
  47.6 1.4 copy.48
  49.6 1.7 select_reduce_fusion.2
  52.1 1.5 fusion.31
  55.1 1.3 select_reduce_fusion.3
  57.2 0.9 select_reduce_fusion.5
  58.9 1.3 fusion.22
  61.9 1.0 fusion.24
  63.7 2.9 squeeze.100
  66.6 1.1 squeeze.101
  67.7 2.2 squeeze.98
  70.0 1.8 select_reduce_fusion.1
  75.6 1.4 convolution_convert_fusion
  77.2 75.3 %reduce-scatter.2.cloned.1.call-done = bf16[96,256]{1,0:T(8,128)(2,1)} async-done(((bf16[96,4096]{1,0:T(8,128)(2,1)}), bf16[96,256]{1,0:T(8,128)(2,1)}) %reduce-scatter.2.cloned.1.call-update) | async-done | bytes 49168 | tf_op jit(solution)/shard_map/reduce_scatter | solution.py:172
  153.4 38.1 %all-reduce = (f32[96]{0:T(128)S(1)}, f32[96]{0:T(128)S(1)}) all-reduce(f32[96]{0:T(128)S(1)} %get-tuple-element.191, f32[96]{0:T(128)S(1)} %get-tuple-element.190), channel_id=1, replica_groups=mesh['group'=8,'tp'=16] {'tp'}, use_global_device_ids=true, to_apply=%region_17.19 | all-reduce | flops 192 | bytes 1536 | tf_op jit(solution)/shard_map/psum | solution.py:176
  192.4 21.9 %all_gather.24 = bf16[96,4096]{1,0:T(8,128)(2,1)S(1)} all-gather(bf16[96,256]{1,0:T(8,128)(2,1)S(1)} %get-tuple-element.211), channel_id=1, replica_groups=mesh['group'=8,'tp'=16] {'tp'}, dimensions={1}, use_global_device_ids=true | all-gather | bytes 835584 | tf_op jit(solution)/shard_map/all_gather | solution.py:180
  214.4 4.7 %add_convert_fusion = bf16[3,96,256]{2,1,0:T(8,128)(2,1)} fusion(bf16[3,4096,256]{2,1,0:T(8,128)(2,1)} %param.25, bf16[96,4096]{1,0:T(8,128)(2,1)S(1)} %all_gather.24, f32[96,256]{1,0:T(8,128)S(1)} %get-tuple-element.210), kind=kOutput, calls=%fused_computation.86 | convolution fusion | flops 604422144 | bytes 7323648 | tf_op jit(solution)/shard_map/td,kdc->ktc/dot_general | solution.py:181
  220.7 9.1 %convolution_bitcast_fusion = f32[1664,1,96]{0,2,1:T(8,128)S(1)} fusion(bf16[96,4096]{1,0:T(8,128)(2,1)S(1)} %all_gather.24, bf16[1664,4096]{1,0:T(8,128)(2,1)} %param.26), kind=kOutput, calls=%fused_computation.23 | convolution fusion | flops 1308622848 | bytes 15056896 | tf_op jit(solution)/shard_map/dot_general | solution.py:186
  229.8 38.5 %all-gather.8.cloned.1.call-done = bf16[3,96,4096]{2,1,0:T(8,128)(2,1)} async-done(((bf16[3,96,256]{2,1,0:T(8,128)(2,1)}), bf16[3,96,4096]{2,1,0:T(8,128)(2,1)}) %all-gather.8.cloned.1.call-update) | async-done | bytes 2359312 | tf_op jit(solution)/shard_map/all_gather | solution.py:192
  268.3 9.1 %fusion.4 = f32[1664,3,96]{0,2,1:T(8,128)S(1)} fusion(bf16[3,96,4096]{2,1,0:T(8,128)(2,1)} %all-gather.8.cloned.1.call-done, bf16[1664,4096]{1,0:T(8,128)(2,1)} %param.26), kind=kOutput, calls=%fused_computation.13 | convolution fusion | flops 3925868544 | bytes 17907712 | tf_op jit(solution)/shard_map/vc,ktc->vkt/dot_general | solution.py:189
  278.9 22.6 %all-gather.5 = f32[16,4,96]{2,1,0:T(4,128)S(1)} all-gather(f32[1,4,96]{2,1,0:T(4,128)S(1)} %bitcast.234), channel_id=4, replica_groups=mesh['group'=8,'tp'=16] {'tp'}, dimensions={0}, use_global_device_ids=true | all-gather | bytes 26112 | tf_op jit(solution)/shard_map/all_gather | solution.py:30
  301.6 21.1 %all-gather.4 = f32[16,4,96]{2,1,0:T(4,128)S(1)} all-gather(f32[1,4,96]{2,1,0:T(4,128)S(1)} %bitcast.233), channel_id=3, replica_groups=mesh['group'=8,'tp'=16] {'tp'}, dimensions={0}, use_global_device_ids=true | all-gather | bytes 26112 | tf_op jit(solution)/shard_map/all_gather | solution.py:30
  322.7 22.6 %all-gather.3 = f32[16,4,96]{2,1,0:T(4,128)S(1)} all-gather(f32[1,4,96]{2,1,0:T(4,128)S(1)} %bitcast.232), channel_id=2, replica_groups=mesh['group'=8,'tp'=16] {'tp'}, dimensions={0}, use_global_device_ids=true | all-gather | bytes 26112 | tf_op jit(solution)/shard_map/all_gather | solution.py:30
  (166 shorter events, 33.7 us)
Async XLA Ops:
  7.2 68.4 %copy-start = (bf16[256,4096]{1,0:T(8,128)(2,1)S(1)}, bf16[256,4096]{1,0:T(8,128)(2,1)}, u32[]{:S(2)}) copy-start(bf16[256,4096]{1,0:T(8,128)(2,1)} %param.23) | copy-start | bytes 6291460
  7.2 145.3 %reduce-scatter.2.cloned.1.call-start = ((), (), s32[]{:S(2)}) async-start(), calls=%async_computation.1 | async-start | bytes 835584 | tf_op jit(solution)/shard_map/reduce_scatter | solution.py:172
  8.8 61.1 %collective-permute-start = (bf16[48,2,128]{2,0,1:T(8,128)(2,1)}, bf16[48,2,128]{2,0,1:T(8,128)(2,1)}, u32[]{:S(2)}, u32[]{:S(2)}) collective-permute-start(bf16[48,2,128]{2,0,1:T(8,128)(2,1)} %copy.49), channel_id=1, source_target_pairs={{0,16},{16,0},{32,48},{48,32},{64,80},{80,64},{96,112},{112,96},{1... | collective-permute-start | bytes 73736 | tf_op jit(solution)/shard_map/ppermute | solution.py:26
  49.6 4.0 %copy-start.5 = (pred[48,48]{0,1:T(8,128)(4,1)S(1)}, pred[48,48]{0,1:T(8,128)(4,1)}, u32[]{:S(2)}) copy-start(pred[48,48]{0,1:T(8,128)(4,1)} %copy.48) | copy-start | bytes 6916
  49.6 4.0 %copy-start.6 = (f32[48,48]{0,1:T(8,128)S(1)}, f32[48,48]{0,1:T(8,128)}, u32[]{:S(2)}) copy-start(f32[48,48]{0,1:T(8,128)} %broadcast_subtract_fusion.3) | copy-start | bytes 27652
  49.6 4.0 %copy-start.7 = (bf16[48,2,128]{2,1,0:T(2,128)(2,1)S(1)}, bf16[48,2,128]{2,1,0:T(2,128)(2,1)}, u32[]{:S(2)}) copy-start(bf16[48,2,128]{2,1,0:T(2,128)(2,1)} %squeeze.94) | copy-start | bytes 73732
  51.3 0.9 copy-start.2
  51.3 3.8 %copy-start.10 = (f32[2,48]{1,0:T(2,128)}, f32[2,48]{1,0:T(2,128)S(1)}, u32[]{:S(2)}) copy-start(f32[2,48]{1,0:T(2,128)S(1)} %get-tuple-element.250) | copy-start | bytes 1156
  54.4 4.4 %copy-start.8 = (f32[2,48]{1,0:T(2,128)}, f32[2,48]{1,0:T(2,128)S(1)}, u32[]{:S(2)}) copy-start(f32[2,48]{1,0:T(2,128)S(1)} %get-tuple-element.248) | copy-start | bytes 1156
  63.6 6.3 %copy-start.12 = (pred[1792]{0:T(1024)(128)(4,1)S(1)}, pred[1792]{0:T(1024)(128)(4,1)}, u32[]{:S(2)}) copy-start(pred[1792]{0:T(1024)(128)(4,1)} %broadcast_compare_fusion.2) | copy-start | bytes 5380
  63.6 6.3 %copy-start.19 = (f32[2]{0:T(128)S(1)}, f32[2]{0:T(128)}, u32[]{:S(2)}) copy-start(f32[2]{0:T(128)} %multiply_exponential_fusion) | copy-start | bytes 28
  69.9 2.8 copy-start.1
  69.9 4.1 %copy-start.9 = (f32[2,48]{1,0:T(2,128)S(1)}, f32[2,48]{1,0:T(2,128)}, u32[]{:S(2)}) copy-start(f32[2,48]{1,0:T(2,128)} %copy-done.8) | copy-start | bytes 1156
  69.9 4.1 %copy-start.11 = (f32[2,48]{1,0:T(2,128)S(1)}, f32[2,48]{1,0:T(2,128)}, u32[]{:S(2)}) copy-start(f32[2,48]{1,0:T(2,128)} %copy-done.10) | copy-start | bytes 1156
  69.9 4.1 %copy-start.14 = (f32[2,48]{1,0:T(2,128)S(1)}, f32[2,48]{1,0:T(2,128)}, u32[]{:S(2)}) copy-start(f32[2,48]{1,0:T(2,128)} %fusion.31) | copy-start | bytes 1156
  69.9 4.9 %copy-start.3 = (f32[2,48,1792]{2,1,0:T(8,128)S(1)}, f32[2,48,1792]{2,1,0:T(8,128)}, u32[]{:S(2)}) copy-start(f32[2,48,1792]{2,1,0:T(8,128)} %copy-done.2) | copy-start | bytes 2064388
  69.9 4.9 %copy-start.13 = (pred[1792]{0:T(1024)(128)(4,1)S(1)}, pred[1792]{0:T(1024)(128)(4,1)}, u32[]{:S(2)}) copy-start(pred[1792]{0:T(1024)(128)(4,1)} %broadcast_compare_fusion.3) | copy-start | bytes 5380
  69.9 4.9 %copy-start.18 = (f32[48,2]{0,1:T(2,128)S(1)}, f32[48,2]{0,1:T(2,128)}, u32[]{:S(2)}) copy-start(f32[48,2]{0,1:T(2,128)} %get-tuple-element.237) | copy-start | bytes 1156
  71.8 2.2 collective-permute-start.1
  72.6 1.3 collective-permute-start.3
  73.4 1.4 collective-permute-start.2
  75.6 76.9 %copy-start.4 = (bf16[96,256]{1,0:T(8,128)(2,1)S(1)}, bf16[96,256]{1,0:T(8,128)(2,1)}, u32[]{:S(2)}) copy-start(bf16[96,256]{1,0:T(8,128)(2,1)} %param.16) | copy-start | bytes 147460
  75.6 116.0 %copy-start.16 = (f32[256]{0:T(256)S(1)}, f32[256]{0:T(256)}, u32[]{:S(2)}) copy-start(f32[256]{0:T(256)} %param.24) | copy-start | bytes 3076
  77.0 191.3 %all-gather.8.cloned.1.call-start = ((), (), s32[]{:S(2)}) async-start(), calls=%async_computation.2 | async-start | bytes 2506752 | tf_op jit(solution)/shard_map/all_gather | solution.py:192
  214.4 4.7 %copy-start.17 = (s32[2,4]{1,0:T(2,128)S(1)}, s32[2,4]{1,0:T(2,128)}, u32[]{:S(2)}) copy-start(s32[2,4]{1,0:T(2,128)} %param.22) | copy-start | bytes 100
  214.4 5.0 %slice-start = ((bf16[3,96,256]{2,1,0:T(8,128)(2,1)}), bf16[2,96,256]{2,1,0:T(8,128)(2,1)S(1)}, s32[]{:S(2)}) async-start(bf16[3,96,256]{2,1,0:T(8,128)(2,1)} %param.17), calls=%async_computation.3 | async-start | bytes 196608 | tf_op jit(solution)/shard_map/slice | solution.py:206
  277.4 0.7 copy-start.15
Sparse Core Ops, SparseCore 0:
  77.1 75.3 reduce-scatter.1
  219.2 49.0 all-gather.7
where the time goes:
time: 355 us; the launch traced here: 353 us
  blocking collectives  126 us (35%)
  waiting for transfers between devices  115 us (32%)
  matrix products  38.7 us (11%)
  local copies, waits for them, and re-layouts  36.3 us (10%)
  other arithmetic  19.1 us (5%)
  between operations  16.6 us (5%)
    reduce_scatter x1, waiting for transfers between devices, shards(): lax.psum_scatter(head_term.astype(jnp.bfloat16), 'tp', scatter_dimension=...  75.3 us
    all_gather x3, blocking collectives, combined_all(): everything = jax.tree.map(lambda part: lax.all_gather(part, axis), array)  66.4 us
    all_gather x1, waiting for transfers between devices, shards(): lax.all_gather(drafted, 'tp', axis=2, tiled=True)  38.5 us
    psum x1, blocking collectives, shards(): lax.psum((jnp.sum(hidden, axis=1), jnp.sum(hidden * hidden, axis=1)), 'tp')  38.1 us
    all_gather x1, blocking collectives, shards(): normed_full = lax.all_gather(normed, 'tp', axis=1, tiled=True)  21.9 us
    dot_general x1, matrix products, shards(): jnp.einsum('vc,ktc->vkt', vocab_weight, lax.all_gather(drafted, 'tp', axi...  9.1 us
    dot_general x1, matrix products, shards(): lax.dot_general(vocab_weight, normed_full, (((1,), (1,)), ((), ())), pref...  9.1 us
  transfers between devices with their start and end apart: 6, of which 3 were waited for; matrix products, arithmetic and copies ran while one was open for 20% of the time, Pallas kernels for 0%

commit v1 on v0

v1 whole, which is shorter than its diff:
```python
import functools
import math

import jax
import jax.numpy as jnp
from jax import lax
from jax.experimental import pallas as pl
from jax.experimental.pallas import tpu as pltpu
from jax.sharding import PartitionSpec as P

D = 4096
HEADS = 32
HD = 128
TREE = 48
SHORT_PAGES = 4
HALF = 14
PAGE = 128
DRAFTS = 3
EPSILON = 1e-05
F32 = jnp.float32
BF16 = jnp.bfloat16
MESH = pl.DeviceIdType.MESH
NT = (((1,), (1,)), ((), ()))


def dot(a, b):
    return jnp.dot(a, b, preferred_element_type=F32)


def dot_nt(a, b):
    return lax.dot_general(a, b, NT, preferred_element_type=F32)


def both_heads(rows):
    lane = lax.broadcasted_iota(jnp.int32, rows.shape, 1)
    zero = jnp.zeros_like(rows)
    return jnp.concatenate(
        [jnp.where(lane < HD, rows, zero), jnp.where(lane >= HD, rows, zero)], axis=0
    )


def own_heads(stacked):
    n = stacked.shape[0] // 2
    return jnp.concatenate([stacked[:n, :HD], stacked[n:, HD:]], axis=1)


def wide(column):
    n = column.shape[0] // 2
    return jnp.concatenate(
        [jnp.broadcast_to(column[:n], (n, HD)), jnp.broadcast_to(column[n:], (n, HD))], axis=1
    )


def row_slopes(lane_index, rows):
    second = lax.broadcasted_iota(jnp.int32, (rows, 1), 0) >= rows // 2
    ordinal = (lane_index * 2 + 1 + jnp.where(second, 1, 0)).astype(F32)
    return jnp.exp2(-8.0 * ordinal / HEADS)


def cache_part(queries, keys, values, slopes, length, first, stride):
    span = keys.shape[0]
    scores = dot_nt(queries, keys) * (1.0 / math.sqrt(HD))
    index = lax.broadcasted_iota(jnp.int32, (1, span), 1)
    place = ((index >> 7) * stride + first) * PAGE + (index & (PAGE - 1))
    relative = place.astype(F32) - length
    exists = relative < 0.0
    scores = jnp.where(exists, scores + slopes * relative, -1e30)
    top = jnp.max(scores, axis=1, keepdims=True)
    weights = jnp.where(exists, jnp.exp(scores - top), 0.0)
    total = jnp.sum(weights, axis=1, keepdims=True)
    return top, total, own_heads(dot(weights.astype(BF16), values))


def join(one, two):
    top = jnp.maximum(one[0], two[0])
    f1, f2 = jnp.exp(one[0] - top), jnp.exp(two[0] - top)
    return top, one[1] * f1 + two[1] * f2, one[2] * wide(f1) + two[2] * wide(f2)


def kernel(
    ntp,
    residual,
    tree,
    pool,
    pages,
    lens,
    parents,
    accepted,
    out_w,
    gain,
    draft_w,
    vocab_w,
    targets,
    probs_out,
    kept_out,
    kbank,
    vbank,
    kbuf,
    vbuf,
    ow,
    dw,
    vw,
    guest_q,
    part_o,
    part_s,
    back_o,
    back_s,
    rs_send,
    rs_got,
    rows_got,
    stat_got,
    normed,
    draft_got,
    logits,
    fin_got,
    square,
    hbm_sem,
    pair_send,
    pair_recv,
    rs_ssem,
    rs_rsem,
    rows_ssem,
    rows_rsem,
    stat_ssem,
    stat_rsem,
    draft_ssem,
    draft_rsem,
    fin_ssem,
    fin_rsem,
):
    g = lax.axis_index("group")
    me = lax.axis_index("tp")
    partner = g + 1 - 2 * lax.rem(g, 2)
    tokens, width = residual.shape
    vocab = vw.shape[0]

    def peer(p):
        return lax.rem(me + p, ntp)

    def cols(t):
        return pl.ds(pl.multiple_of(t * width, width), width)

    def to(src, dst, ssem, rsem, where):
        return pltpu.make_async_remote_copy(
            src_ref=src, dst_ref=dst, send_sem=ssem, recv_sem=rsem, device_id=where, device_id_type=MESH
        )

    def load(src, dst, k):
        return pltpu.make_async_copy(src, dst, hbm_sem.at[k])

    load_k = load(pool.at[0], kbank, 0)
    load_v = load(pool.at[1], vbank, 1)
    load_o = load(out_w, ow, 2)
    load_d = load(draft_w, dw, 3)
    load_w = load(vocab_w, vw, 4)
    load_k.start()
    load_v.start()

    barrier = pltpu.get_barrier_semaphore()
    pl.semaphore_signal(barrier, inc=1, device_id=(partner, me), device_id_type=MESH)

    @pl.loop(1, ntp)
    def _(p):
        pl.semaphore_signal(barrier, inc=1, device_id=(g, peer(p)), device_id_type=MESH)

    parent = parents[pl.ds(g, 1), :]
    sub = lax.broadcasted_iota(jnp.int32, (tokens, tokens), 0)
    lan = lax.broadcasted_iota(jnp.int32, (tokens, tokens), 1)
    base = jnp.where(lan >= TREE, TREE, 0)
    linked = (parent + base == sub) & (lan != base)
    up = jnp.where(linked | (sub == lan), 1.0, 0.0).astype(BF16)
    for _ in range(TREE.bit_length()):
        up = jnp.minimum(dot(up, up), 1.0).astype(BF16)
    up32 = up.astype(F32)
    depth = jnp.sum(up32, axis=0, keepdims=True) - 1.0
    square[...] = jnp.zeros_like(square)
    square[0:tokens, 0:tokens] = up32
    ancestor = square[...].T[0:tokens, 0:tokens]

    row = lax.broadcasted_iota(jnp.int32, (16, tokens), 0)
    col = lax.broadcasted_iota(jnp.int32, (16, tokens), 1)
    pick = jnp.zeros((16, tokens), jnp.bool_)
    for i in range(8):
        pick = pick | ((row == i) & (col == (i // 4) * TREE + accepted[i // 4, i % 4]))
    chosen = jnp.where(pick, 1.0, 0.0).astype(BF16)
    for c in range(2):
        kept_out[c] = dot(chosen, tree[c + 1])[0:8].astype(BF16)

    pl.semaphore_wait(barrier, ntp)
    ask = to(tree.at[0, pl.ds(TREE, TREE)], guest_q, pair_send.at[0], pair_recv.at[0], (partner, me))
    ask.start()

    slopes = row_slopes(me, 2 * TREE)
    mine, guest = 2 * g + 1, 2 * partner + 1

    load_k.wait()
    load_o.start()
    load_d.start()

    def collect(bank, buf):
        for start, count, request, first, stride in (
            (0, HALF, guest, 1, 2),
            (HALF, HALF, mine, 0, 2),
            (2 * HALF, SHORT_PAGES, 2 * g, 0, 1),
        ):

            @pl.loop(0, count)
            def _(i):
                buf[pl.ds(pl.multiple_of((start + i) * PAGE, PAGE), PAGE), :] = bank[
                    pages[request, first + stride * i]
                ]

    collect(kbank, kbuf)
    load_v.wait()
    load_w.start()
    collect(vbank, vbuf)

    def over(first, count):
        return pl.ds(first * PAGE, count * PAGE)

    ask.wait_recv()
    top, total, out = cache_part(
        both_heads(guest_q[...]),
        kbuf[over(0, HALF)],
        vbuf[over(0, HALF)],
        slopes,
        lens[guest].astype(F32),
        1,
        2,
    )
    part_o[...] = out
    lane = lax.broadcasted_iota(jnp.int32, (2 * TREE, 128), 1)
    part_s[...] = jnp.where(lane < 64, top, total)
    give_o = to(part_o, back_o, pair_send.at[1], pair_recv.at[1], (partner, me))
    give_s = to(part_s, back_s, pair_send.at[2], pair_recv.at[2], (partner, me))
    give_o.start()
    give_s.start()

    long_part = cache_part(
        both_heads(tree[0, TREE : 2 * TREE]),
        kbuf[over(HALF, HALF)],
        vbuf[over(HALF, HALF)],
        slopes,
        lens[mine].astype(F32),
        0,
        2,
    )
    short_part = cache_part(
        both_heads(tree[0, 0:TREE]),
        kbuf[over(2 * HALF, SHORT_PAGES)],
        vbuf[over(2 * HALF, SHORT_PAGES)],
        slopes,
        lens[2 * g].astype(F32),
        0,
        1,
    )

    seen = jnp.concatenate([ancestor, ancestor], axis=0) > 0.5
    scores = dot_nt(both_heads(tree[0]), tree[1]) * (1.0 / math.sqrt(HD))
    scores = jnp.where(seen, scores + row_slopes(me, 2 * tokens) * depth, -1e30)
    top = jnp.max(scores, axis=1, keepdims=True)
    weights = jnp.where(seen, jnp.exp(scores - top), 0.0)
    total = jnp.sum(weights, axis=1, keepdims=True)
    out = own_heads(dot(weights.astype(BF16), tree[2]))

    def of_request(r):
        at = r * TREE
        return (
            jnp.concatenate([top[at : at + TREE], top[tokens + at : tokens + at + TREE]], 0),
            jnp.concatenate([total[at : at + TREE], total[tokens + at : tokens + at + TREE]], 0),
            out[at : at + TREE],
        )

    short = join(of_request(0), short_part)
    long = join(of_request(1), long_part)
    give_o.wait_recv()
    give_s.wait_recv()
    back = back_s[...]
    long = join(long, (back[:, 0:1], back[:, 64:65], back_o[...]))
    attn = jnp.concatenate([short[2] / wide(short[1]), long[2] / wide(long[1])], 0).astype(BF16)

    load_o.wait()

    @pl.loop(1, ntp)
    def _(p):
        t = peer(p)
        rs_send[t] = dot(attn, ow[:, cols(t)]).astype(BF16)
        to(rs_send.at[t], rs_got.at[me], rs_ssem.at[t], rs_rsem.at[me], (g, t)).start()

    hidden = residual[...].astype(F32) + dot(attn, ow[:, cols(me)])

    def add_share(p, so_far):
        s = peer(p)
        to(rs_send.at[s], rs_got.at[s], rs_ssem.at[s], rs_rsem.at[s], (g, s)).wait_recv()
        return so_far + rs_got[s].astype(F32)

    hidden = lax.fori_loop(1, ntp, add_share, hidden)

    block_sum = jnp.sum(hidden, axis=1, keepdims=True)
    block_square = jnp.sum(hidden * hidden, axis=1, keepdims=True)
    block_mean = block_sum * (1.0 / width)
    rows_got[me] = (hidden - block_mean).astype(BF16)
    lane = lax.broadcasted_iota(jnp.int32, (tokens, 128), 1)
    square[0:tokens, :] = jnp.where(
        lane == 0, block_sum, jnp.where(lane == 1, block_square, jnp.where(lane == 2, block_mean, 0.0))
    )
    stat_got[me] = square[...].T[0:8]
    stat_got[me, 4:6, :] = gain[...]

    @pl.loop(1, ntp)
    def _(p):
        t = peer(p)
        to(stat_got.at[me], stat_got.at[me], stat_ssem.at[t], stat_rsem.at[me], (g, t)).start()
        to(rows_got.at[me], rows_got.at[me], rows_ssem.at[t], rows_rsem.at[me], (g, t)).start()

    @pl.loop(1, ntp)
    def _(p):
        s = peer(p)
        to(stat_got.at[s], stat_got.at[s], stat_ssem.at[s], stat_rsem.at[s], (g, s)).wait_recv()
        to(rows_got.at[s], rows_got.at[s], rows_ssem.at[s], rows_rsem.at[s], (g, s)).wait_recv()

    stats = stat_got[...].reshape(128, 128).T[0:tokens]
    mean = jnp.sum(jnp.where(lane % 8 == 0, stats, 0.0), axis=1, keepdims=True) * (1.0 / D)
    spread = jnp.sum(jnp.where(lane % 8 == 1, stats, 0.0), axis=1, keepdims=True) * (1.0 / D)
    scale = lax.rsqrt(spread - mean * mean + EPSILON)
    for s in range(ntp):
        shift = stats[:, 8 * s + 2 : 8 * s + 3] - mean
        gains = jnp.concatenate([stat_got[s, 4:5, :], stat_got[s, 5:6, :]], axis=1)
        normed[:, s * width : (s + 1) * width] = (
            (rows_got[s].astype(F32) + shift) * scale * gains
        ).astype(BF16)

    load_d.wait()
    own_rows = normed[:, cols(me)].astype(F32)
    for k in range(DRAFTS):
        update = dot(normed[...], dw[k])
        draft_got[k, :, cols(me)] = (own_rows + update / (1.0 + jnp.exp(-update))).astype(BF16)

        @pl.loop(1, ntp)
        def _(p):
            t = peer(p)
            here = draft_got.at[k, :, cols(me)]
            to(here, here, draft_ssem.at[k, t], draft_rsem.at[k, me], (g, t)).start()

    load_w.wait()
    step = 256
    whole = vocab // step

    def some_logits(rows, first):
        def block(at, n):
            logits[first : first + rows.shape[0], pl.ds(at, n)] = dot_nt(rows, vw[pl.ds(at, n), :])

        @pl.loop(0, whole)
        def _(i):
            block(pl.multiple_of(i * step, step), step)

        if vocab > whole * step:
            block(whole * step, vocab - whole * step)

    some_logits(normed[...], 0)

    square[...] = jnp.zeros_like(square)
    square[0:4, 0:tokens] = targets[...].astype(F32)
    wanted = square[...].T[0:tokens]

    for k in range(DRAFTS):

        @pl.loop(1, ntp)
        def _(p):
            s = peer(p)
            there = draft_got.at[k, :, cols(s)]
            to(there, there, draft_ssem.at[k, s], draft_rsem.at[k, s], (g, s)).wait_recv()

    some_logits(draft_got[...].reshape(DRAFTS * tokens, D), tokens)

    entry = (lax.broadcasted_iota(jnp.int32, (1, vocab), 1) + me * vocab).astype(F32)
    summary = jnp.zeros((tokens, 128), F32)
    for k in range(DRAFTS + 1):
        x = logits[k * tokens : (k + 1) * tokens, :]
        top = jnp.max(x, axis=1, keepdims=True)
        total = jnp.sum(jnp.exp(x - top), axis=1, keepdims=True)
        picked = jnp.sum(jnp.where(entry == wanted[:, k : k + 1], x, 0.0), axis=1, keepdims=True)
        for c, value in enumerate((top, total, picked)):
            summary = jnp.where(lane == 8 * c + k, value, summary)
    square[0:tokens, :] = summary
    fin_got[me] = square[...].T[0:24]

    @pl.loop(1, ntp)
    def _(p):
        t = peer(p)
        to(fin_got.at[me], fin_got.at[me], fin_ssem.at[t], fin_rsem.at[me], (g, t)).start()

    ask.wait_send()
    give_o.wait_send()
    give_s.wait_send()

    @pl.loop(1, ntp)
    def _(p):
        t = peer(p)
        to(rs_send.at[t], rs_got.at[me], rs_ssem.at[t], rs_rsem.at[me], (g, t)).wait_send()
        to(stat_got.at[me], stat_got.at[me], stat_ssem.at[t], stat_rsem.at[me], (g, t)).wait_send()
        to(rows_got.at[me], rows_got.at[me], rows_ssem.at[t], rows_rsem.at[me], (g, t)).wait_send()
        for k in range(DRAFTS):
            here = draft_got.at[k, :, cols(me)]
            to(here, here, draft_ssem.at[k, t], draft_rsem.at[k, me], (g, t)).wait_send()

    @pl.loop(1, ntp)
    def _(p):
        s = peer(p)
        to(fin_got.at[s], fin_got.at[s], fin_ssem.at[s], fin_rsem.at[s], (g, s)).wait_recv()

    tops, totals, picks = fin_got[:, 0:8, :], fin_got[:, 8:16, :], fin_got[:, 16:24, :]
    top = jnp.max(tops, axis=0)
    total = jnp.sum(totals * jnp.exp(tops - top[None]), axis=0)
    answer = jnp.sum(picks, axis=0) - (top + jnp.log(total))
    probs_out[...] = answer[0:4, 0:tokens]

    @pl.loop(1, ntp)
    def _(p):
        t = peer(p)
        to(fin_got.at[me], fin_got.at[me], fin_ssem.at[t], fin_rsem.at[me], (g, t)).wait_send()


def shards(ntp, *args):
    (
        residual,
        tree_qkv,
        kv_pool,
        page_table,
        cache_len,
        tree_parent,
        accepted_nodes,
        out_weight,
        norm_gain,
        draft_weight,
        vocab_weight,
        target_ids,
    ) = args
    tokens, width = residual.shape
    slots = kv_pool.shape[1]
    used = (2 * HALF + SHORT_PAGES) * PAGE
    vmem = pl.BlockSpec(memory_space=pltpu.VMEM)
    smem = pl.BlockSpec(memory_space=pltpu.SMEM)
    anywhere = pl.BlockSpec(memory_space=pl.ANY)
    dma = pltpu.SemaphoreType.DMA
    return pl.pallas_call(
        functools.partial(kernel, ntp),
        out_shape=(
            jax.ShapeDtypeStruct((DRAFTS + 1, tokens), F32),
            jax.ShapeDtypeStruct((2, 8, width), BF16),
        ),
        in_specs=[vmem, vmem, anywhere, smem, smem, vmem, smem, anywhere, vmem, anywhere, anywhere, vmem],
        out_specs=(vmem, vmem),
        scratch_shapes=[
            pltpu.VMEM((slots, PAGE, width), BF16),
            pltpu.VMEM((slots, PAGE, width), BF16),
            pltpu.VMEM((used, width), BF16),
            pltpu.VMEM((used, width), BF16),
            pltpu.VMEM((width, D), BF16),
            pltpu.VMEM((DRAFTS, D, width), BF16),
            pltpu.VMEM(vocab_weight.shape, BF16),
            pltpu.VMEM((TREE, width), BF16),
            pltpu.VMEM((TREE, width), F32),
            pltpu.VMEM((2 * TREE, 128), F32),
            pltpu.VMEM((TREE, width), F32),
            pltpu.VMEM((2 * TREE, 128), F32),
            pltpu.VMEM((ntp, tokens, width), BF16),
            pltpu.VMEM((ntp, tokens, width), BF16),
            pltpu.VMEM((ntp, tokens, width), BF16),
            pltpu.VMEM((ntp, 8, 128), F32),
            pltpu.VMEM((tokens, D), BF16),
            pltpu.VMEM((DRAFTS, tokens, D), BF16),
            pltpu.VMEM(((DRAFTS + 1) * tokens, vocab_weight.shape[0]), F32),
            pltpu.VMEM((ntp, 24, 128), F32),
            pltpu.VMEM((128, 128), F32),
            dma((5,)),
            dma((3,)),
            dma((3,)),
            dma((ntp,)),
            dma((ntp,)),
            dma((ntp,)),
            dma((ntp,)),
            dma((ntp,)),
            dma((ntp,)),
            dma((DRAFTS, ntp)),
            dma((DRAFTS, ntp)),
            dma((ntp,)),
            dma((ntp,)),
        ],
        compiler_params=pltpu.CompilerParams(
            collective_id=0, has_side_effects=True, vmem_limit_bytes=60 * 1024 * 1024
        ),
        cost_estimate=pl.CostEstimate(flops=6_200_000_000, bytes_accessed=27_000_000, transcendentals=1_000_000),
    )(
        residual,
        tree_qkv,
        kv_pool,
        page_table,
        cache_len,
        tree_parent.reshape(-1, 2 * TREE),
        accepted_nodes,
        out_weight,
        norm_gain.reshape(2, width // 2),
        draft_weight,
        vocab_weight,
        target_ids,
    )


def solution(mesh):
    placed = (
        P("group", "tp"),
        P(None, "group", "tp"),
        P(None, "group", None, "tp"),
        P(),
        P(),
        P(),
        P("group", None),
        P("tp", None),
        P("tp"),
        P(None, None, "tp"),
        P("tp", None),
        P(None, "group"),
    )
    return jax.shard_map(
        functools.partial(shards, mesh.shape["tp"]),
        mesh=mesh,
        in_specs=placed,
        out_specs=(P(None, "group"), P(None, "group", "tp")),
        check_vma=False,
    )
```

time: 355 us -> 86.5 us (0.24)
  blocking collectives: 126 us -> 0 us
  waiting for transfers between devices: 115 us -> 0 us
  Pallas kernels: 0 us -> 81.8 us
  matrix products: 38.7 us -> 0 us
  local copies, waits for them, and re-layouts: 36.3 us -> 3.89 us
  other arithmetic: 19.1 us -> 0 us
  between operations: 16.6 us -> 0.64 us
    all_gather x4 -> x0, blocking collectives: 88.3 us -> none  [the longest x3 66.4 us: combined_all(): everything = jax.tree.map(lambda part: lax.all_gather(part, axis), array)]
    pallas_call x0 -> x1, Pallas kernels: none -> 81.8 us  [shards(): pl.pallas_call(functools.partial(kernel, ntp), out_shape=(jax.ShapeDtypeS...]
    reduce_scatter x1 -> x0, waiting for transfers between devices: 75.3 us -> none  [shards(): lax.psum_scatter(head_term.astype(jnp.bfloat16), 'tp', scatter_dimension=...]
    dot_general x32 -> x0, matrix products: 38.7 us -> none  [the longest x1 9.1 us: shards(): jnp.einsum('vc,ktc->vkt', vocab_weight, lax.all_gather(drafted, 'tp', axi...]
    all_gather x1 -> x0, waiting for transfers between devices: 38.5 us -> none  [shards(): lax.all_gather(drafted, 'tp', axis=2, tiled=True)]
    psum x1 -> x0, blocking collectives: 38.1 us -> none  [shards(): lax.psum((jnp.sum(hidden, axis=1), jnp.sum(hidden * hidden, axis=1)), 'tp')]
    squeeze x13 -> x0, local copies, waits for them, and re-layouts: 13.8 us -> none  [the longest x3 6.62 us: page_attention(): flat_pages[0]]
    gather x4 -> x0, local copies, waits for them, and re-layouts: 11.6 us -> none  [the longest x2 6.9 us: shards(): own_pages = jnp.take(kv_pool, own_slots, axis=1)]
  transfers between devices with their start and end apart: 6 -> 0, of which waited for: 3 -> 0; matrix products, arithmetic and copies ran while one was open for 20% -> 0% of each run, Pallas kernels for 0% -> 0%
where the time goes in v1:
time: 86.5 us; the launch traced here: 86.3 us
  Pallas kernels  81.8 us (95%)
  local copies, waits for them, and re-layouts  3.89 us (4%)
    pallas_call x1, Pallas kernels, shards(): pl.pallas_call(functools.partial(kernel, ntp), out_shape=(jax.ShapeDtypeS...  81.8 us
    unnamed x2, local copies, waits for them, and re-layouts  2.53 us

profile of v1, /device:TPU:0, one launch (start us, length us, event | category | flops | bytes accessed | tf_op | source)
XLA Modules:
  0.0 86.3 jit_solution(10737721211889251109)
XLA Ops:
  0.6 1.4 %reshape.10.parents = s32[8,96]{1,0:T(8,128)} reshape(s32[16,48]{1,0:T(8,128)} %param.17) | data formatting | bytes 6144 | tf_op jit(solution)/shard_map/reshape | solution.py:500
  2.0 81.8 %shard_map.131 = (f32[4,96]{1,0:T(4,128)}, bf16[2,8,256]{2,1,0:T(8,128)(2,1)}) custom-call(bf16[96,256]{1,0:T(8,128)(2,1)} %residual.1, bf16[3,96,256]{2,1,0:T(8,128)(2,1)} %tree.1, bf16[2,32,128,256]{3,2,1,0:T(8,128)(2,1)} %pool.1, s32[16,28]{1,0:T(8,128)} %pages.1, s32[16]{0:T(128)} %lens.1, s32[8,96]{1,0:T(8,128)} %reshape.10.parents, s32[2,4]{1,0:T(2,128)} %accepted.1, ...), custom_call_target="tpu_custom_call" | custom-call | flops 6200000000 | bytes 27000000 | tf_op jit(solution)/shard_map/pallas_call | solution.py:446
  83.8 1.2 %copy.16 = f32[4,96]{1,0:T(4,128)} copy(f32[4,96]{1,0:T(4,128)} %get-tuple-element.4) | data formatting | bytes 3072
  85.0 1.3 %copy.17 = bf16[2,8,256]{2,1,0:T(8,128)(2,1)} copy(bf16[2,8,256]{2,1,0:T(8,128)(2,1)} %get-tuple-element.5) | data formatting | bytes 16384

commit v2 on v1

--- a/solution.py
+++ b/solution.py
@@ -140,6 +140,14 @@
     def cols(t):
         return pl.ds(pl.multiple_of(t * width, width), width)
 
+    side = math.isqrt(ntp)
+    mx, mz = me // side, lax.rem(me, side)
+
+    def hop(axis, by):
+        if axis == 0:
+            return (g, lax.rem(mx + by, side) * side + mz)
+        return (g, mx * side + lax.rem(mz + by, side))
+
     def to(src, dst, ssem, rsem, where):
         return pltpu.make_async_remote_copy(
             src_ref=src, dst_ref=dst, send_sem=ssem, recv_sem=rsem, device_id=where, device_id_type=MESH
@@ -163,7 +171,7 @@
     def _(p):
         pl.semaphore_signal(barrier, inc=1, device_id=(g, peer(p)), device_id_type=MESH)
 
-    parent = parents[pl.ds(g, 1), :]
+    parent = jnp.concatenate([parents[pl.ds(2 * g, 1), :], parents[pl.ds(2 * g + 1, 1), :]], axis=1)
     sub = lax.broadcasted_iota(jnp.int32, (tokens, tokens), 0)
     lan = lax.broadcasted_iota(jnp.int32, (tokens, tokens), 1)
     base = jnp.where(lan >= TREE, TREE, 0)
@@ -330,48 +338,108 @@
             (rows_got[s].astype(F32) + shift) * scale * gains
         ).astype(BF16)
 
+    halves = (pl.ds(0, tokens // 2), pl.ds(tokens // 2, tokens // 2))
+
+    def line(half, k, at, some=slice(None)):
+        if half == 0:
+            return draft_got.at[some, at, k, halves[0]]
+        return draft_got.at[at, some, k, halves[1]]
+
+    def pairs(k, base, moves):
+        made = []
+        for j, (sent, got, where) in enumerate(moves):
+            sems = draft_ssem.at[k, base + j], draft_rsem.at[k, base + j]
+            made.append(
+                (functools.partial(to, sent, sent, *sems, where), functools.partial(to, got, got, *sems, where))
+            )
+        return made
+
+    def place(half, along, across):
+        a, b = lax.rem((mx, mz)[half] + along, side), lax.rem((mx, mz)[1 - half] + across, side)
+        return (a, b) if half == 0 else (b, a)
+
+    def first_phase(k):
+        moves = []
+        for by in (1, side - 1, 2):
+            for half in range(2):
+                own = draft_got.at[mx, mz, k, halves[half]]
+                x, z = place(half, side - by, 0)
+                moves.append((own, draft_got.at[x, z, k, halves[half]], hop(half, by)))
+        return pairs(k, 0, moves)
+
+    def second_phase(k):
+        moves = []
+        for by in (1, side - 1):
+            for half in range(2):
+                mid = (mx, mz)[1 - half]
+                got = line(half, k, lax.rem(mid + side - by, side))
+                moves.append((line(half, k, mid), got, hop(1 - half, by)))
+        return pairs(k, 6, moves)
+
+    def third_phase(k):
+        moves = []
+        for by, some in ((1, pl.ds(0, side // 2)), (side - 1, pl.ds(side // 2, side // 2))):
+            for half in range(2):
+                mid = (mx, mz)[1 - half]
+                sent = line(half, k, lax.rem(mid + side - by, side), some)
+                got = line(half, k, lax.rem(mid + 2, side), some)
+                moves.append((sent, got, hop(1 - half, by)))
+        return pairs(k, 10, moves)
+
+    def follow(arrived, onward):
+        for _, copy in arrived:
+            copy().wait_recv()
+        for copy, _ in onward:
+            copy().start()
+
     load_d.wait()
     own_rows = normed[:, cols(me)].astype(F32)
     for k in range(DRAFTS):
         update = dot(normed[...], dw[k])
-        draft_got[k, :, cols(me)] = (own_rows + update / (1.0 + jnp.exp(-update))).astype(BF16)
-
-        @pl.loop(1, ntp)
-        def _(p):
-            t = peer(p)
-            here = draft_got.at[k, :, cols(me)]
-            to(here, here, draft_ssem.at[k, t], draft_rsem.at[k, me], (g, t)).start()
+        draft_got[mx, mz, k] = (own_rows + update / (1.0 + jnp.exp(-update))).astype(BF16)
+        for copy, _ in first_phase(k):
+            copy().start()
 
     load_w.wait()
     step = 256
     whole = vocab // step
 
-    def some_logits(rows, first):
-        def block(at, n):
-            logits[first : first + rows.shape[0], pl.ds(at, n)] = dot_nt(rows, vw[pl.ds(at, n), :])
-
-        @pl.loop(0, whole)
-        def _(i):
-            block(pl.multiple_of(i * step, step), step)
-
-        if vocab > whole * step:
-            block(whole * step, vocab - whole * step)
-
-    some_logits(normed[...], 0)
+    tiles = [(i * step, step) for i in range(whole)]
+    if vocab > whole * step:
+        tiles.append((whole * step, vocab - whole * step))
+
+    def base_logits(i):
+        at, n = tiles[i]
+        logits[0:tokens, at : at + n] = dot_nt(normed[...], vw[at : at + n, :])
+
+    events = [(first_phase(k), second_phase(k)) for k in range(DRAFTS)]
+    events += [(second_phase(k), third_phase(k)) for k in range(DRAFTS)]
+    for i in range(max(len(tiles), len(events))):
+        if i < len(tiles):
+            base_logits(i)
+        if i < len(events):
+            follow(*events[i])
 
     square[...] = jnp.zeros_like(square)
     square[0:4, 0:tokens] = targets[...].astype(F32)
     wanted = square[...].T[0:tokens]
 
     for k in range(DRAFTS):
-
-        @pl.loop(1, ntp)
-        def _(p):
-            s = peer(p)
-            there = draft_got.at[k, :, cols(s)]
-            to(there, there, draft_ssem.at[k, s], draft_rsem.at[k, s], (g, s)).wait_recv()
-
-    some_logits(draft_got[...].reshape(DRAFTS * tokens, D), tokens)
+        follow(third_phase(k), ())
+
+    def draft_logits(at, n):
+        total = jnp.zeros((DRAFTS * tokens, n), F32)
+        for t in range(ntp):
+            rows = draft_got[t // side, t % side].reshape(DRAFTS * tokens, width)
+            total += dot_nt(rows, vw[pl.ds(at, n), t * width : (t + 1) * width])
+        logits[tokens : (DRAFTS + 1) * tokens, pl.ds(at, n)] = total
+
+    @pl.loop(0, whole)
+    def _(i):
+        draft_logits(pl.multiple_of(i * step, step), step)
+
+    if vocab > whole * step:
+        draft_logits(whole * step, vocab - whole * step)
 
     entry = (lax.broadcasted_iota(jnp.int32, (1, vocab), 1) + me * vocab).astype(F32)
     summary = jnp.zeros((tokens, 128), F32)
@@ -390,6 +458,9 @@
         t = peer(p)
         to(fin_got.at[me], fin_got.at[me], fin_ssem.at[t], fin_rsem.at[me], (g, t)).start()
 
+    for k in range(DRAFTS):
+        for copy, _ in first_phase(k) + second_phase(k) + third_phase(k):
+            copy().wait_send()
     ask.wait_send()
     give_o.wait_send()
     give_s.wait_send()
@@ -400,9 +471,6 @@
         to(rs_send.at[t], rs_got.at[me], rs_ssem.at[t], rs_rsem.at[me], (g, t)).wait_send()
         to(stat_got.at[me], stat_got.at[me], stat_ssem.at[t], stat_rsem.at[me], (g, t)).wait_send()
         to(rows_got.at[me], rows_got.at[me], rows_ssem.at[t], rows_rsem.at[me], (g, t)).wait_send()
-        for k in range(DRAFTS):
-            here = draft_got.at[k, :, cols(me)]
-            to(here, here, draft_ssem.at[k, t], draft_rsem.at[k, me], (g, t)).wait_send()
 
     @pl.loop(1, ntp)
     def _(p):
@@ -438,6 +506,7 @@
     ) = args
     tokens, width = residual.shape
     slots = kv_pool.shape[1]
+    side = math.isqrt(ntp)
     used = (2 * HALF + SHORT_PAGES) * PAGE
     vmem = pl.BlockSpec(memory_space=pltpu.VMEM)
     smem = pl.BlockSpec(memory_space=pltpu.SMEM)
@@ -469,7 +538,7 @@
             pltpu.VMEM((ntp, tokens, width), BF16),
             pltpu.VMEM((ntp, 8, 128), F32),
             pltpu.VMEM((tokens, D), BF16),
-            pltpu.VMEM((DRAFTS, tokens, D), BF16),
+            pltpu.VMEM((side, side, DRAFTS, tokens, width), BF16),
             pltpu.VMEM(((DRAFTS + 1) * tokens, vocab_weight.shape[0]), F32),
             pltpu.VMEM((ntp, 24, 128), F32),
             pltpu.VMEM((128, 128), F32),
@@ -482,8 +551,8 @@
             dma((ntp,)),
             dma((ntp,)),
             dma((ntp,)),
-            dma((DRAFTS, ntp)),
-            dma((DRAFTS, ntp)),
+            dma((DRAFTS, 14)),
+            dma((DRAFTS, 14)),
             dma((ntp,)),
             dma((ntp,)),
         ],
@@ -497,7 +566,7 @@
         kv_pool,
         page_table,
         cache_len,
-        tree_parent.reshape(-1, 2 * TREE),
+        tree_parent,
         accepted_nodes,
         out_weight,
         norm_gain.reshape(2, width // 2),

time: 86.5 us -> 74.2 us (0.86)
  Pallas kernels: 81.8 us -> 70.8 us
  local copies, waits for them, and re-layouts: 3.89 us -> 2.53 us
    pallas_call x1, Pallas kernels: 81.8 us -> 70.8 us  [shards(): pl.pallas_call(functools.partial(kernel, ntp), out_shape=(jax.ShapeDtypeS...]
    reshape x1 -> x0, local copies, waits for them, and re-layouts: 1.36 us -> none  [shards(): tree_parent.reshape(-1, 2 * TREE)]
where the time goes in v2:
time: 74.2 us; the launch traced here: 74 us
  Pallas kernels  70.8 us (95%)
  local copies, waits for them, and re-layouts  2.53 us (3%)
    pallas_call x1, Pallas kernels, shards(): pl.pallas_call(functools.partial(kernel, ntp), out_shape=(jax.ShapeDtypeS...  70.8 us
    unnamed x2, local copies, waits for them, and re-layouts  2.53 us

profile of v2, /device:TPU:0, one launch (start us, length us, event | category | flops | bytes accessed | tf_op | source)
XLA Modules:
  0.0 74.0 jit_solution(435119531554017562)
XLA Ops:
  0.6 70.8 %shard_map.131 = (f32[4,96]{1,0:T(4,128)}, bf16[2,8,256]{2,1,0:T(8,128)(2,1)}) custom-call(bf16[96,256]{1,0:T(8,128)(2,1)} %residual.1, bf16[3,96,256]{2,1,0:T(8,128)(2,1)} %tree.1, bf16[2,32,128,256]{3,2,1,0:T(8,128)(2,1)} %pool.1, s32[16,28]{1,0:T(8,128)} %pages.1, s32[16]{0:T(128)} %lens.1, s32[16,48]{1,0:T(8,128)} %parents.1, s32[2,4]{1,0:T(2,128)} %accepted.1, ...), custom_call_target="tpu_custom_call" | custom-call | flops 6200000000 | bytes 27000000 | tf_op jit(solution)/shard_map/pallas_call | solution.py:515
  71.4 1.2 %copy.16 = f32[4,96]{1,0:T(4,128)} copy(f32[4,96]{1,0:T(4,128)} %get-tuple-element.4) | data formatting | bytes 3072
  72.7 1.3 %copy.17 = bf16[2,8,256]{2,1,0:T(8,128)(2,1)} copy(bf16[2,8,256]{2,1,0:T(8,128)(2,1)} %get-tuple-element.5) | data formatting | bytes 16384

commit v3 on v2

--- a/solution.py
+++ b/solution.py
@@ -226,6 +226,46 @@
     def over(first, count):
         return pl.ds(first * PAGE, count * PAGE)
 
+    short_part = cache_part(
+        both_heads(tree[0, 0:TREE]),
+        kbuf[over(2 * HALF, SHORT_PAGES)],
+        vbuf[over(2 * HALF, SHORT_PAGES)],
+        slopes,
+        lens[2 * g].astype(F32),
+        0,
+        1,
+    )
+
+    seen = jnp.concatenate([ancestor, ancestor], axis=0) > 0.5
+    scores = dot_nt(both_heads(tree[0]), tree[1]) * (1.0 / math.sqrt(HD))
+    scores = jnp.where(seen, scores + row_slopes(me, 2 * tokens) * depth, -1e30)
+    top = jnp.max(scores, axis=1, keepdims=True)
+    weights = jnp.where(seen, jnp.exp(scores - top), 0.0)
+    total = jnp.sum(weights, axis=1, keepdims=True)
+    out = own_heads(dot(weights.astype(BF16), tree[2]))
+
+    def of_request(r):
+        at = r * TREE
+        return (
+            jnp.concatenate([top[at : at + TREE], top[tokens + at : tokens + at + TREE]], 0),
+            jnp.concatenate([total[at : at + TREE], total[tokens + at : tokens + at + TREE]], 0),
+            out[at : at + TREE],
+        )
+
+    def project(h, merged):
+        attn = (merged[2] / wide(merged[1])).astype(BF16)
+        for t in range(ntp):
+            rs_send[h, t] = dot(attn, ow[:, t * width : (t + 1) * width]).astype(BF16)
+
+        @pl.loop(1, ntp)
+        def _(p):
+            t = peer(p)
+            to(rs_send.at[h, t], rs_got.at[h, me], rs_ssem.at[h, t], rs_rsem.at[h, me], (g, t)).start()
+
+    load_o.wait()
+    project(0, join(of_request(0), short_part))
+    long = of_request(1)
+
     ask.wait_recv()
     top, total, out = cache_part(
         both_heads(guest_q[...]),
@@ -253,138 +293,96 @@
         0,
         2,
     )
-    short_part = cache_part(
-        both_heads(tree[0, 0:TREE]),
-        kbuf[over(2 * HALF, SHORT_PAGES)],
-        vbuf[over(2 * HALF, SHORT_PAGES)],
-        slopes,
-        lens[2 * g].astype(F32),
-        0,
-        1,
-    )
-
-    seen = jnp.concatenate([ancestor, ancestor], axis=0) > 0.5
-    scores = dot_nt(both_heads(tree[0]), tree[1]) * (1.0 / math.sqrt(HD))
-    scores = jnp.where(seen, scores + row_slopes(me, 2 * tokens) * depth, -1e30)
-    top = jnp.max(scores, axis=1, keepdims=True)
-    weights = jnp.where(seen, jnp.exp(scores - top), 0.0)
-    total = jnp.sum(weights, axis=1, keepdims=True)
-    out = own_heads(dot(weights.astype(BF16), tree[2]))
-
-    def of_request(r):
-        at = r * TREE
-        return (
-            jnp.concatenate([top[at : at + TREE], top[tokens + at : tokens + at + TREE]], 0),
-            jnp.concatenate([total[at : at + TREE], total[tokens + at : tokens + at + TREE]], 0),
-            out[at : at + TREE],
-        )
-
-    short = join(of_request(0), short_part)
-    long = join(of_request(1), long_part)
+    long = join(long, long_part)
     give_o.wait_recv()
     give_s.wait_recv()
     back = back_s[...]
-    long = join(long, (back[:, 0:1], back[:, 64:65], back_o[...]))
-    attn = jnp.concatenate([short[2] / wide(short[1]), long[2] / wide(long[1])], 0).astype(BF16)
-
-    load_o.wait()
-
-    @pl.loop(1, ntp)
-    def _(p):
-        t = peer(p)
-        rs_send[t] = dot(attn, ow[:, cols(t)]).astype(BF16)
-        to(rs_send.at[t], rs_got.at[me], rs_ssem.at[t], rs_rsem.at[me], (g, t)).start()
-
-    hidden = residual[...].astype(F32) + dot(attn, ow[:, cols(me)])
-
-    def add_share(p, so_far):
-        s = peer(p)
-        to(rs_send.at[s], rs_got.at[s], rs_ssem.at[s], rs_rsem.at[s], (g, s)).wait_recv()
-        return so_far + rs_got[s].astype(F32)
-
-    hidden = lax.fori_loop(1, ntp, add_share, hidden)
-
-    block_sum = jnp.sum(hidden, axis=1, keepdims=True)
-    block_square = jnp.sum(hidden * hidden, axis=1, keepdims=True)
-    block_mean = block_sum * (1.0 / width)
-    rows_got[me] = (hidden - block_mean).astype(BF16)
-    lane = lax.broadcasted_iota(jnp.int32, (tokens, 128), 1)
-    square[0:tokens, :] = jnp.where(
-        lane == 0, block_sum, jnp.where(lane == 1, block_square, jnp.where(lane == 2, block_mean, 0.0))
-    )
-    stat_got[me] = square[...].T[0:8]
-    stat_got[me, 4:6, :] = gain[...]
-
-    @pl.loop(1, ntp)
-    def _(p):
-        t = peer(p)
-        to(stat_got.at[me], stat_got.at[me], stat_ssem.at[t], stat_rsem.at[me], (g, t)).start()
-        to(rows_got.at[me], rows_got.at[me], rows_ssem.at[t], rows_rsem.at[me], (g, t)).start()
-
-    @pl.loop(1, ntp)
-    def _(p):
-        s = peer(p)
-        to(stat_got.at[s], stat_got.at[s], stat_ssem.at[s], stat_rsem.at[s], (g, s)).wait_recv()
-        to(rows_got.at[s], rows_got.at[s], rows_ssem.at[s], rows_rsem.at[s], (g, s)).wait_recv()
-
-    stats = stat_got[...].reshape(128, 128).T[0:tokens]
-    mean = jnp.sum(jnp.where(lane % 8 == 0, stats, 0.0), axis=1, keepdims=True) * (1.0 / D)
-    spread = jnp.sum(jnp.where(lane % 8 == 1, stats, 0.0), axis=1, keepdims=True) * (1.0 / D)
-    scale = lax.rsqrt(spread - mean * mean + EPSILON)
-    for s in range(ntp):
-        shift = stats[:, 8 * s + 2 : 8 * s + 3] - mean
-        gains = jnp.concatenate([stat_got[s, 4:5, :], stat_got[s, 5:6, :]], axis=1)
-        normed[:, s * width : (s + 1) * width] = (
-            (rows_got[s].astype(F32) + shift) * scale * gains
-        ).astype(BF16)
-
-    halves = (pl.ds(0, tokens // 2), pl.ds(tokens // 2, tokens // 2))
+    project(1, join(long, (back[:, 0:1], back[:, 64:65], back_o[...])))
+
+    lane = lax.broadcasted_iota(jnp.int32, (TREE, 128), 1)
+
+    def share_rows(h):
+        def add_share(p, so_far):
+            s = peer(p)
+            to(rs_send.at[h, s], rs_got.at[h, s], rs_ssem.at[h, s], rs_rsem.at[h, s], (g, s)).wait_recv()
+            return so_far + rs_got[h, s].astype(F32)
+
+        hidden = residual[h * TREE : (h + 1) * TREE, :].astype(F32) + rs_send[h, me].astype(F32)
+        hidden = lax.fori_loop(1, ntp, add_share, hidden)
+        block_sum = jnp.sum(hidden, axis=1, keepdims=True)
+        block_square = jnp.sum(hidden * hidden, axis=1, keepdims=True)
+        block_mean = block_sum * (1.0 / width)
+        rows_got[h, me] = (hidden - block_mean).astype(BF16)
+        square[0:TREE, :] = jnp.where(
+            lane == 0, block_sum, jnp.where(lane == 1, block_square, jnp.where(lane == 2, block_mean, 0.0))
+        )
+        stat_got[h, me] = square[...].T[0:8]
+        stat_got[h, me, 4:6, :] = gain[...]
+
+        @pl.loop(1, ntp)
+        def _(p):
+            t = peer(p)
+            stat, rows = stat_got.at[h, me], rows_got.at[h, me]
+            to(stat, stat, stat_ssem.at[h, t], stat_rsem.at[h, me], (g, t)).start()
+            to(rows, rows, rows_ssem.at[h, t], rows_rsem.at[h, me], (g, t)).start()
+
+    def normalise(h):
+        @pl.loop(1, ntp)
+        def _(p):
+            s = peer(p)
+            stat, rows = stat_got.at[h, s], rows_got.at[h, s]
+            to(stat, stat, stat_ssem.at[h, s], stat_rsem.at[h, s], (g, s)).wait_recv()
+            to(rows, rows, rows_ssem.at[h, s], rows_rsem.at[h, s], (g, s)).wait_recv()
+
+        stats = stat_got[h].reshape(128, 128).T[0:TREE]
+        mean = jnp.sum(jnp.where(lane % 8 == 0, stats, 0.0), axis=1, keepdims=True) * (1.0 / D)
+        spread = jnp.sum(jnp.where(lane % 8 == 1, stats, 0.0), axis=1, keepdims=True) * (1.0 / D)
+        scale = lax.rsqrt(spread - mean * mean + EPSILON)
+        for s in range(ntp):
+            shift = stats[:, 8 * s + 2 : 8 * s + 3] - mean
+            gains = jnp.concatenate([stat_got[h, s, 4:5, :], stat_got[h, s, 5:6, :]], axis=1)
+            normed[h * TREE : (h + 1) * TREE, s * width : (s + 1) * width] = (
+                (rows_got[h, s].astype(F32) + shift) * scale * gains
+            ).astype(BF16)
 
     def line(half, k, at, some=slice(None)):
-        if half == 0:
-            return draft_got.at[some, at, k, halves[0]]
-        return draft_got.at[at, some, k, halves[1]]
-
-    def pairs(k, base, moves):
+        rows = pl.ds(half * TREE, TREE)
+        return draft_got.at[some, at, k, rows] if half == 0 else draft_got.at[at, some, k, rows]
+
+    def pairs(half, k, base, moves):
         made = []
         for j, (sent, got, where) in enumerate(moves):
-            sems = draft_ssem.at[k, base + j], draft_rsem.at[k, base + j]
+            sems = draft_ssem.at[half, k, base + j], draft_rsem.at[half, k, base + j]
             made.append(
                 (functools.partial(to, sent, sent, *sems, where), functools.partial(to, got, got, *sems, where))
             )
         return made
 
-    def place(half, along, across):
-        a, b = lax.rem((mx, mz)[half] + along, side), lax.rem((mx, mz)[1 - half] + across, side)
-        return (a, b) if half == 0 else (b, a)
-
-    def first_phase(k):
+    def first_phase(half, k):
         moves = []
+        rows = pl.ds(half * TREE, TREE)
         for by in (1, side - 1, 2):
-            for half in range(2):
-                own = draft_got.at[mx, mz, k, halves[half]]
-                x, z = place(half, side - by, 0)
-                moves.append((own, draft_got.at[x, z, k, halves[half]], hop(half, by)))
-        return pairs(k, 0, moves)
-
-    def second_phase(k):
+            from_there = lax.rem((mx, mz)[half] + side - by, side)
+            x, z = (from_there, mz) if half == 0 else (mx, from_there)
+            moves.append((draft_got.at[mx, mz, k, rows], draft_got.at[x, z, k, rows], hop(half, by)))
+        return pairs(half, k, 0, moves)
+
+    def second_phase(half, k):
         moves = []
+        mid = (mx, mz)[1 - half]
         for by in (1, side - 1):
-            for half in range(2):
-                mid = (mx, mz)[1 - half]
-                got = line(half, k, lax.rem(mid + side - by, side))
-                moves.append((line(half, k, mid), got, hop(1 - half, by)))
-        return pairs(k, 6, moves)
-
-    def third_phase(k):
+            got = line(half, k, lax.rem(mid + side - by, side))
+            moves.append((line(half, k, mid), got, hop(1 - half, by)))
+        return pairs(half, k, 3, moves)
+
+    def third_phase(half, k):
         moves = []
+        mid = (mx, mz)[1 - half]
         for by, some in ((1, pl.ds(0, side // 2)), (side - 1, pl.ds(side // 2, side // 2))):
-            for half in range(2):
-                mid = (mx, mz)[1 - half]
-                sent = line(half, k, lax.rem(mid + side - by, side), some)
-                got = line(half, k, lax.rem(mid + 2, side), some)
-                moves.append((sent, got, hop(1 - half, by)))
-        return pairs(k, 10, moves)
+            sent = line(half, k, lax.rem(mid + side - by, side), some)
+            got = line(half, k, lax.rem(mid + 2, side), some)
+            moves.append((sent, got, hop(1 - half, by)))
+        return pairs(half, k, 5, moves)
 
     def follow(arrived, onward):
         for _, copy in arrived:
@@ -392,13 +390,33 @@
         for copy, _ in onward:
             copy().start()
 
+    def one_two(half, k):
+        follow(first_phase(half, k), second_phase(half, k))
+
+    def two_three(half, k):
+        follow(second_phase(half, k), third_phase(half, k))
+
+    def draft(h, k):
+        rows = slice(h * TREE, (h + 1) * TREE)
+        update = dot(normed[rows, :], dw[k])
+        own_rows = normed[rows, cols(me)].astype(F32)
+        draft_got[mx, mz, k, rows, :] = (own_rows + update / (1.0 + jnp.exp(-update))).astype(BF16)
+        follow((), first_phase(h, k))
+
+    share_rows(0)
+    share_rows(1)
+    normalise(0)
     load_d.wait()
-    own_rows = normed[:, cols(me)].astype(F32)
     for k in range(DRAFTS):
-        update = dot(normed[...], dw[k])
-        draft_got[mx, mz, k] = (own_rows + update / (1.0 + jnp.exp(-update))).astype(BF16)
-        for copy, _ in first_phase(k):
-            copy().start()
+        draft(0, k)
+    one_two(0, 0)
+    one_two(0, 1)
+    normalise(1)
+    draft(1, 0)
+    one_two(0, 2)
+    draft(1, 1)
+    two_three(0, 0)
+    draft(1, 2)
 
     load_w.wait()
     step = 256
@@ -412,20 +430,30 @@
         at, n = tiles[i]
         logits[0:tokens, at : at + n] = dot_nt(normed[...], vw[at : at + n, :])
 
-    events = [(first_phase(k), second_phase(k)) for k in range(DRAFTS)]
-    events += [(second_phase(k), third_phase(k)) for k in range(DRAFTS)]
+    events = (
+        (one_two, 1, 0),
+        (two_three, 0, 1),
+        (one_two, 1, 1),
+        (two_three, 0, 2),
+        (one_two, 1, 2),
+        (two_three, 1, 0),
+        (two_three, 1, 1),
+        (two_three, 1, 2),
+    )
     for i in range(max(len(tiles), len(events))):
         if i < len(tiles):
             base_logits(i)
         if i < len(events):
-            follow(*events[i])
+            event, half, k = events[i]
+            event(half, k)
 
     square[...] = jnp.zeros_like(square)
     square[0:4, 0:tokens] = targets[...].astype(F32)
     wanted = square[...].T[0:tokens]
 
     for k in range(DRAFTS):
-        follow(third_phase(k), ())
+        for half in range(2):
+            follow(third_phase(half, k), ())
 
     def draft_logits(at, n):
         total = jnp.zeros((DRAFTS * tokens, n), F32)
@@ -443,6 +471,7 @@
 
     entry = (lax.broadcasted_iota(jnp.int32, (1, vocab), 1) + me * vocab).astype(F32)
     summary = jnp.zeros((tokens, 128), F32)
+    lane = lax.broadcasted_iota(jnp.int32, (tokens, 128), 1)
     for k in range(DRAFTS + 1):
         x = logits[k * tokens : (k + 1) * tokens, :]
         top = jnp.max(x, axis=1, keepdims=True)
@@ -459,8 +488,9 @@
         to(fin_got.at[me], fin_got.at[me], fin_ssem.at[t], fin_rsem.at[me], (g, t)).start()
 
     for k in range(DRAFTS):
-        for copy, _ in first_phase(k) + second_phase(k) + third_phase(k):
-            copy().wait_send()
+        for half in range(2):
+            for copy, _ in first_phase(half, k) + second_phase(half, k) + third_phase(half, k):
+                copy().wait_send()
     ask.wait_send()
     give_o.wait_send()
     give_s.wait_send()
@@ -468,9 +498,11 @@
     @pl.loop(1, ntp)
     def _(p):
         t = peer(p)
-        to(rs_send.at[t], rs_got.at[me], rs_ssem.at[t], rs_rsem.at[me], (g, t)).wait_send()
-        to(stat_got.at[me], stat_got.at[me], stat_ssem.at[t], stat_rsem.at[me], (g, t)).wait_send()
-        to(rows_got.at[me], rows_got.at[me], rows_ssem.at[t], rows_rsem.at[me], (g, t)).wait_send()
+        for h in range(2):
+            stat, rows = stat_got.at[h, me], rows_got.at[h, me]
+            to(rs_send.at[h, t], rs_got.at[h, me], rs_ssem.at[h, t], rs_rsem.at[h, me], (g, t)).wait_send()
+            to(stat, stat, stat_ssem.at[h, t], stat_rsem.at[h, me], (g, t)).wait_send()
+            to(rows, rows, rows_ssem.at[h, t], rows_rsem.at[h, me], (g, t)).wait_send()
 
     @pl.loop(1, ntp)
     def _(p):
@@ -533,10 +565,10 @@
             pltpu.VMEM((2 * TREE, 128), F32),
             pltpu.VMEM((TREE, width), F32),
             pltpu.VMEM((2 * TREE, 128), F32),
-            pltpu.VMEM((ntp, tokens, width), BF16),
-            pltpu.VMEM((ntp, tokens, width), BF16),
-            pltpu.VMEM((ntp, tokens, width), BF16),
-            pltpu.VMEM((ntp, 8, 128), F32),
+            pltpu.VMEM((2, ntp, TREE, width), BF16),
+            pltpu.VMEM((2, ntp, TREE, width), BF16),
+            pltpu.VMEM((2, ntp, TREE, width), BF16),
+            pltpu.VMEM((2, ntp, 8, 128), F32),
             pltpu.VMEM((tokens, D), BF16),
             pltpu.VMEM((side, side, DRAFTS, tokens, width), BF16),
             pltpu.VMEM(((DRAFTS + 1) * tokens, vocab_weight.shape[0]), F32),
@@ -545,14 +577,14 @@
             dma((5,)),
             dma((3,)),
             dma((3,)),
-            dma((ntp,)),
-            dma((ntp,)),
-            dma((ntp,)),
-            dma((ntp,)),
-            dma((ntp,)),
-            dma((ntp,)),
-            dma((DRAFTS, 14)),
-            dma((DRAFTS, 14)),
+            dma((2, ntp)),
+            dma((2, ntp)),
+            dma((2, ntp)),
+            dma((2, ntp)),
+            dma((2, ntp)),
+            dma((2, ntp)),
+            dma((2, DRAFTS, 7)),
+            dma((2, DRAFTS, 7)),
             dma((ntp,)),
             dma((ntp,)),
         ],

time: 74.2 us -> 72.8 us (0.981)
  Pallas kernels: 70.8 us -> 69.4 us
    pallas_call x1, Pallas kernels: 70.8 us -> 69.4 us  [shards(): pl.pallas_call(functools.partial(kernel, ntp), out_shape=(jax.ShapeDtypeS...]
where the time goes in v3:
time: 72.8 us; the launch traced here: 72.6 us
  Pallas kernels  69.4 us (95%)
  local copies, waits for them, and re-layouts  2.53 us (3%)
    pallas_call x1, Pallas kernels, shards(): pl.pallas_call(functools.partial(kernel, ntp), out_shape=(jax.ShapeDtypeS...  69.4 us
    unnamed x2, local copies, waits for them, and re-layouts  2.53 us

profile of v3, /device:TPU:0, one launch (start us, length us, event | category | flops | bytes accessed | tf_op | source)
XLA Modules:
  0.0 72.6 jit_solution(8519276844454489743)
XLA Ops:
  0.6 69.4 %shard_map.131 = (f32[4,96]{1,0:T(4,128)}, bf16[2,8,256]{2,1,0:T(8,128)(2,1)}) custom-call(bf16[96,256]{1,0:T(8,128)(2,1)} %residual.1, bf16[3,96,256]{2,1,0:T(8,128)(2,1)} %tree.1, bf16[2,32,128,256]{3,2,1,0:T(8,128)(2,1)} %pool.1, s32[16,28]{1,0:T(8,128)} %pages.1, s32[16]{0:T(128)} %lens.1, s32[16,48]{1,0:T(8,128)} %parents.1, s32[2,4]{1,0:T(2,128)} %accepted.1, ...), custom_call_target="tpu_custom_call" | custom-call | flops 6200000000 | bytes 27000000 | tf_op jit(solution)/shard_map/pallas_call | solution.py:547
  70.1 1.2 %copy.16 = f32[4,96]{1,0:T(4,128)} copy(f32[4,96]{1,0:T(4,128)} %get-tuple-element.4) | data formatting | bytes 3072
  71.3 1.3 %copy.17 = bf16[2,8,256]{2,1,0:T(8,128)(2,1)} copy(bf16[2,8,256]{2,1,0:T(8,128)(2,1)} %get-tuple-element.5) | data formatting | bytes 16384

commit v4 on v3

--- a/solution.py
+++ b/solution.py
@@ -107,10 +107,9 @@
     back_s,
     rs_send,
     rs_got,
-    rows_got,
     stat_got,
     normed,
-    draft_got,
+    spread,
     logits,
     fin_got,
     square,
@@ -119,12 +118,10 @@
     pair_recv,
     rs_ssem,
     rs_rsem,
-    rows_ssem,
-    rows_rsem,
     stat_ssem,
     stat_rsem,
-    draft_ssem,
-    draft_rsem,
+    ring_ssem,
+    ring_rsem,
     fin_ssem,
     fin_rsem,
 ):
@@ -299,6 +296,73 @@
     back = back_s[...]
     project(1, join(long, (back[:, 0:1], back[:, 64:65], back_o[...])))
 
+    half_width = width // 2
+    here = (mx, mz)
+
+    def line(item, half, at, some=slice(None)):
+        return spread.at[item, half, some, at] if half == 0 else spread.at[item, half, at, some]
+
+    def moves(item, half, base, made):
+        out = []
+        for j, (sent, got, where) in enumerate(made):
+            sems = ring_ssem.at[item, half, base + j], ring_rsem.at[item, half, base + j]
+            out.append(
+                (functools.partial(to, sent, sent, *sems, where), functools.partial(to, got, got, *sems, where))
+            )
+        return out
+
+    def first_phase(item):
+        out = []
+        for half in range(2):
+            made = []
+            for by in (1, side - 1, 2):
+                other = lax.rem(here[half] + side - by, side)
+                x, z = (other, mz) if half == 0 else (mx, other)
+                made.append((spread.at[item, half, mx, mz], spread.at[item, half, x, z], hop(half, by)))
+            out += moves(item, half, 0, made)
+        return out
+
+    def second_phase(item):
+        out = []
+        for half in range(2):
+            mid = here[1 - half]
+            made = []
+            for by in (1, side - 1) + ((2,) if item < 2 else ()):
+                got = line(item, half, lax.rem(mid + side - by, side))
+                made.append((line(item, half, mid), got, hop(1 - half, by)))
+            out += moves(item, half, 3, made)
+        return out
+
+    def third_phase(item):
+        out = []
+        for half in range(2):
+            mid = here[1 - half]
+            made = []
+            for by, some in ((1, pl.ds(0, side // 2)), (side - 1, pl.ds(side // 2, side // 2))):
+                sent = line(item, half, lax.rem(mid + side - by, side), some)
+                got = line(item, half, lax.rem(mid + 2, side), some)
+                made.append((sent, got, hop(1 - half, by)))
+            out += moves(item, half, 5, made)
+        return out
+
+    def follow(arrived, onward):
+        for _, copy in arrived:
+            copy().wait_recv()
+        for copy, _ in onward:
+            copy().start()
+
+    def one_two(item):
+        follow(first_phase(item), second_phase(item))
+
+    def two_three(item):
+        follow(second_phase(item), third_phase(item))
+
+    def publish(item, rows):
+        rows = rows.astype(BF16)
+        for half in range(2):
+            spread[item, half, mx, mz] = rows[:, half * half_width : (half + 1) * half_width]
+        follow((), first_phase(item))
+
     lane = lax.broadcasted_iota(jnp.int32, (TREE, 128), 1)
 
     def share_rows(h):
@@ -312,7 +376,6 @@
         block_sum = jnp.sum(hidden, axis=1, keepdims=True)
         block_square = jnp.sum(hidden * hidden, axis=1, keepdims=True)
         block_mean = block_sum * (1.0 / width)
-        rows_got[h, me] = (hidden - block_mean).astype(BF16)
         square[0:TREE, :] = jnp.where(
             lane == 0, block_sum, jnp.where(lane == 1, block_square, jnp.where(lane == 2, block_mean, 0.0))
         )
@@ -322,101 +385,60 @@
         @pl.loop(1, ntp)
         def _(p):
             t = peer(p)
-            stat, rows = stat_got.at[h, me], rows_got.at[h, me]
+            stat = stat_got.at[h, me]
             to(stat, stat, stat_ssem.at[h, t], stat_rsem.at[h, me], (g, t)).start()
-            to(rows, rows, rows_ssem.at[h, t], rows_rsem.at[h, me], (g, t)).start()
+
+        publish(h, hidden - block_mean)
 
     def normalise(h):
         @pl.loop(1, ntp)
         def _(p):
             s = peer(p)
-            stat, rows = stat_got.at[h, s], rows_got.at[h, s]
+            stat = stat_got.at[h, s]
             to(stat, stat, stat_ssem.at[h, s], stat_rsem.at[h, s], (g, s)).wait_recv()
-            to(rows, rows, rows_ssem.at[h, s], rows_rsem.at[h, s], (g, s)).wait_recv()
+
+        follow(second_phase(h), ())
 
         stats = stat_got[h].reshape(128, 128).T[0:TREE]
         mean = jnp.sum(jnp.where(lane % 8 == 0, stats, 0.0), axis=1, keepdims=True) * (1.0 / D)
-        spread = jnp.sum(jnp.where(lane % 8 == 1, stats, 0.0), axis=1, keepdims=True) * (1.0 / D)
-        scale = lax.rsqrt(spread - mean * mean + EPSILON)
+        squares = jnp.sum(jnp.where(lane % 8 == 1, stats, 0.0), axis=1, keepdims=True) * (1.0 / D)
+        scale = lax.rsqrt(squares - mean * mean + EPSILON)
         for s in range(ntp):
             shift = stats[:, 8 * s + 2 : 8 * s + 3] - mean
             gains = jnp.concatenate([stat_got[h, s, 4:5, :], stat_got[h, s, 5:6, :]], axis=1)
+            rows = jnp.concatenate([spread[h, half, s // side, s % side] for half in range(2)], axis=1)
             normed[h * TREE : (h + 1) * TREE, s * width : (s + 1) * width] = (
-                (rows_got[h, s].astype(F32) + shift) * scale * gains
+                (rows.astype(F32) + shift) * scale * gains
             ).astype(BF16)
-
-    def line(half, k, at, some=slice(None)):
-        rows = pl.ds(half * TREE, TREE)
-        return draft_got.at[some, at, k, rows] if half == 0 else draft_got.at[at, some, k, rows]
-
-    def pairs(half, k, base, moves):
-        made = []
-        for j, (sent, got, where) in enumerate(moves):
-            sems = draft_ssem.at[half, k, base + j], draft_rsem.at[half, k, base + j]
-            made.append(
-                (functools.partial(to, sent, sent, *sems, where), functools.partial(to, got, got, *sems, where))
-            )
-        return made
-
-    def first_phase(half, k):
-        moves = []
-        rows = pl.ds(half * TREE, TREE)
-        for by in (1, side - 1, 2):
-            from_there = lax.rem((mx, mz)[half] + side - by, side)
-            x, z = (from_there, mz) if half == 0 else (mx, from_there)
-            moves.append((draft_got.at[mx, mz, k, rows], draft_got.at[x, z, k, rows], hop(half, by)))
-        return pairs(half, k, 0, moves)
-
-    def second_phase(half, k):
-        moves = []
-        mid = (mx, mz)[1 - half]
-        for by in (1, side - 1):
-            got = line(half, k, lax.rem(mid + side - by, side))
-            moves.append((line(half, k, mid), got, hop(1 - half, by)))
-        return pairs(half, k, 3, moves)
-
-    def third_phase(half, k):
-        moves = []
-        mid = (mx, mz)[1 - half]
-        for by, some in ((1, pl.ds(0, side // 2)), (side - 1, pl.ds(side // 2, side // 2))):
-            sent = line(half, k, lax.rem(mid + side - by, side), some)
-            got = line(half, k, lax.rem(mid + 2, side), some)
-            moves.append((sent, got, hop(1 - half, by)))
-        return pairs(half, k, 5, moves)
-
-    def follow(arrived, onward):
-        for _, copy in arrived:
-            copy().wait_recv()
-        for copy, _ in onward:
-            copy().start()
-
-    def one_two(half, k):
-        follow(first_phase(half, k), second_phase(half, k))
-
-    def two_three(half, k):
-        follow(second_phase(half, k), third_phase(half, k))
 
     def draft(h, k):
         rows = slice(h * TREE, (h + 1) * TREE)
         update = dot(normed[rows, :], dw[k])
         own_rows = normed[rows, cols(me)].astype(F32)
-        draft_got[mx, mz, k, rows, :] = (own_rows + update / (1.0 + jnp.exp(-update))).astype(BF16)
-        follow((), first_phase(h, k))
+        publish(2 + 2 * k + h, own_rows + update / (1.0 + jnp.exp(-update)))
+
+    def item(h, k):
+        return 2 + 2 * k + h
 
     share_rows(0)
+    one_two(0)
     share_rows(1)
     normalise(0)
     load_d.wait()
-    for k in range(DRAFTS):
-        draft(0, k)
-    one_two(0, 0)
-    one_two(0, 1)
+    draft(0, 0)
+    one_two(1)
+    draft(0, 1)
+    draft(0, 2)
+    one_two(item(0, 0))
     normalise(1)
     draft(1, 0)
-    one_two(0, 2)
+    one_two(item(0, 1))
     draft(1, 1)
-    two_three(0, 0)
+    one_two(item(0, 2))
+    two_three(item(0, 0))
     draft(1, 2)
+    one_two(item(1, 0))
+    two_three(item(0, 1))
 
     load_w.wait()
     step = 256
@@ -431,43 +453,61 @@
         logits[0:tokens, at : at + n] = dot_nt(normed[...], vw[at : at + n, :])
 
     events = (
-        (one_two, 1, 0),
-        (two_three, 0, 1),
-        (one_two, 1, 1),
-        (two_three, 0, 2),
-        (one_two, 1, 2),
-        (two_three, 1, 0),
-        (two_three, 1, 1),
-        (two_three, 1, 2),
+        ((one_two, 1, 1), (two_three, 0, 2)),
+        ((one_two, 1, 2),),
+        ((two_three, 1, 0),),
+        (),
+        ((two_three, 1, 1),),
+        (),
+        ((two_three, 1, 2),),
     )
     for i in range(max(len(tiles), len(events))):
         if i < len(tiles):
             base_logits(i)
         if i < len(events):
-            event, half, k = events[i]
-            event(half, k)
+            for event, h, k in events[i]:
+                event(item(h, k))
 
     square[...] = jnp.zeros_like(square)
     square[0:4, 0:tokens] = targets[...].astype(F32)
     wanted = square[...].T[0:tokens]
 
+    drafts = DRAFTS * tokens
+
+    def some_drafts(at, n, lines):
+        total = jnp.zeros((drafts, n), F32)
+        for half in range(2):
+            for by in lines:
+                mid = lax.rem(here[1 - half] + by, side)
+                for first in range(0, side, 2):
+                    rows, weights = [], []
+                    for other in (first, first + 1):
+                        x, z = (other, mid) if half == 0 else (mid, other)
+                        rows.append(spread[2 : 2 * (DRAFTS + 1), half, x, z].reshape(drafts, half_width))
+                        place = (x * side + z) * width + half * half_width
+                        weights.append(vw[pl.ds(at, n), pl.ds(pl.multiple_of(place, half_width), half_width)])
+                    total += dot_nt(jnp.concatenate(rows, axis=1), jnp.concatenate(weights, axis=1))
+        return total
+
+    def each_tile(body):
+        @pl.loop(0, whole)
+        def _(i):
+            body(pl.multiple_of(i * step, step), step)
+
+        if vocab > whole * step:
+            body(whole * step, vocab - whole * step)
+
+    def near(at, n):
+        logits[tokens : tokens + drafts, pl.ds(at, n)] = some_drafts(at, n, (0, 1, side - 1))
+
+    def far(at, n):
+        logits[tokens : tokens + drafts, pl.ds(at, n)] += some_drafts(at, n, (2,))
+
+    each_tile(near)
     for k in range(DRAFTS):
-        for half in range(2):
-            follow(third_phase(half, k), ())
-
-    def draft_logits(at, n):
-        total = jnp.zeros((DRAFTS * tokens, n), F32)
-        for t in range(ntp):
-            rows = draft_got[t // side, t % side].reshape(DRAFTS * tokens, width)
-            total += dot_nt(rows, vw[pl.ds(at, n), t * width : (t + 1) * width])
-        logits[tokens : (DRAFTS + 1) * tokens, pl.ds(at, n)] = total
-
-    @pl.loop(0, whole)
-    def _(i):
-        draft_logits(pl.multiple_of(i * step, step), step)
-
-    if vocab > whole * step:
-        draft_logits(whole * step, vocab - whole * step)
+        for h in range(2):
+            follow(third_phase(item(h, k)), ())
+    each_tile(far)
 
     entry = (lax.broadcasted_iota(jnp.int32, (1, vocab), 1) + me * vocab).astype(F32)
     summary = jnp.zeros((tokens, 128), F32)
@@ -487,10 +527,9 @@
         t = peer(p)
         to(fin_got.at[me], fin_got.at[me], fin_ssem.at[t], fin_rsem.at[me], (g, t)).start()
 
-    for k in range(DRAFTS):
-        for half in range(2):
-            for copy, _ in first_phase(half, k) + second_phase(half, k) + third_phase(half, k):
-                copy().wait_send()
+    for i in range(2 * (DRAFTS + 1)):
+        for copy, _ in first_phase(i) + second_phase(i) + (third_phase(i) if i >= 2 else []):
+            copy().wait_send()
     ask.wait_send()
     give_o.wait_send()
     give_s.wait_send()
@@ -499,10 +538,9 @@
     def _(p):
         t = peer(p)
         for h in range(2):
-            stat, rows = stat_got.at[h, me], rows_got.at[h, me]
+            stat = stat_got.at[h, me]
             to(rs_send.at[h, t], rs_got.at[h, me], rs_ssem.at[h, t], rs_rsem.at[h, me], (g, t)).wait_send()
             to(stat, stat, stat_ssem.at[h, t], stat_rsem.at[h, me], (g, t)).wait_send()
-            to(rows, rows, rows_ssem.at[h, t], rows_rsem.at[h, me], (g, t)).wait_send()
 
     @pl.loop(1, ntp)
     def _(p):
@@ -567,10 +605,9 @@
             pltpu.VMEM((2 * TREE, 128), F32),
             pltpu.VMEM((2, ntp, TREE, width), BF16),
             pltpu.VMEM((2, ntp, TREE, width), BF16),
-            pltpu.VMEM((2, ntp, TREE, width), BF16),
             pltpu.VMEM((2, ntp, 8, 128), F32),
             pltpu.VMEM((tokens, D), BF16),
-            pltpu.VMEM((side, side, DRAFTS, tokens, width), BF16),
+            pltpu.VMEM((2 * (DRAFTS + 1), 2, side, side, TREE, width // 2), BF16),
             pltpu.VMEM(((DRAFTS + 1) * tokens, vocab_weight.shape[0]), F32),
             pltpu.VMEM((ntp, 24, 128), F32),
             pltpu.VMEM((128, 128), F32),
@@ -581,10 +618,8 @@
             dma((2, ntp)),
             dma((2, ntp)),
             dma((2, ntp)),
-            dma((2, ntp)),
-            dma((2, ntp)),
-            dma((2, DRAFTS, 7)),
-            dma((2, DRAFTS, 7)),
+            dma((2 * (DRAFTS + 1), 2, 7)),
+            dma((2 * (DRAFTS + 1), 2, 7)),
             dma((ntp,)),
             dma((ntp,)),
         ],

time: 72.8 us -> 68.2 us (0.937)
  Pallas kernels: 69.4 us -> 64.9 us
    pallas_call x1, Pallas kernels: 69.4 us -> 64.9 us  [shards(): pl.pallas_call(functools.partial(kernel, ntp), out_shape=(jax.ShapeDtypeS...]
where the time goes in v4:
time: 68.2 us; the launch traced here: 68 us
  Pallas kernels  64.9 us (95%)
  local copies, waits for them, and re-layouts  2.53 us (4%)
    pallas_call x1, Pallas kernels, shards(): pl.pallas_call(functools.partial(kernel, ntp), out_shape=(jax.ShapeDtypeS...  64.9 us
    unnamed x2, local copies, waits for them, and re-layouts  2.53 us

profile of v4, /device:TPU:0, one launch (start us, length us, event | category | flops | bytes accessed | tf_op | source)
XLA Modules:
  0.0 68.0 jit_solution(11944016235660518214)
XLA Ops:
  0.6 64.9 %shard_map.131 = (f32[4,96]{1,0:T(4,128)}, bf16[2,8,256]{2,1,0:T(8,128)(2,1)}) custom-call(bf16[96,256]{1,0:T(8,128)(2,1)} %residual.1, bf16[3,96,256]{2,1,0:T(8,128)(2,1)} %tree.1, bf16[2,32,128,256]{3,2,1,0:T(8,128)(2,1)} %pool.1, s32[16,28]{1,0:T(8,128)} %pages.1, s32[16]{0:T(128)} %lens.1, s32[16,48]{1,0:T(8,128)} %parents.1, s32[2,4]{1,0:T(2,128)} %accepted.1, ...), custom_call_target="tpu_custom_call" | custom-call | flops 6200000000 | bytes 27000000 | tf_op jit(solution)/shard_map/pallas_call | solution.py:585
  65.5 1.2 %copy.16 = f32[4,96]{1,0:T(4,128)} copy(f32[4,96]{1,0:T(4,128)} %get-tuple-element.4) | data formatting | bytes 3072
  66.8 1.3 %copy.17 = bf16[2,8,256]{2,1,0:T(8,128)(2,1)} copy(bf16[2,8,256]{2,1,0:T(8,128)(2,1)} %get-tuple-element.5) | data formatting | bytes 16384

commit v5 on v4

--- a/solution.py
+++ b/solution.py
@@ -17,6 +17,7 @@
 PAGE = 128
 DRAFTS = 3
 EPSILON = 1e-05
+ROUTED = (0, 1, 3, 5, 7)
 F32 = jnp.float32
 BF16 = jnp.bfloat16
 MESH = pl.DeviceIdType.MESH
@@ -108,7 +109,7 @@
     rs_send,
     rs_got,
     stat_got,
-    normed,
+    acts,
     spread,
     logits,
     fin_got,
@@ -158,8 +159,8 @@
     load_o = load(out_w, ow, 2)
     load_d = load(draft_w, dw, 3)
     load_w = load(vocab_w, vw, 4)
-    load_k.start()
-    load_v.start()
+    for copy in (load_k, load_v, load_o, load_d, load_w):
+        copy.start()
 
     barrier = pltpu.get_barrier_semaphore()
     pl.semaphore_signal(barrier, inc=1, device_id=(partner, me), device_id_type=MESH)
@@ -199,8 +200,6 @@
     mine, guest = 2 * g + 1, 2 * partner + 1
 
     load_k.wait()
-    load_o.start()
-    load_d.start()
 
     def collect(bank, buf):
         for start, count, request, first, stride in (
@@ -209,15 +208,11 @@
             (2 * HALF, SHORT_PAGES, 2 * g, 0, 1),
         ):
 
-            @pl.loop(0, count)
-            def _(i):
-                buf[pl.ds(pl.multiple_of((start + i) * PAGE, PAGE), PAGE), :] = bank[
-                    pages[request, first + stride * i]
-                ]
+            for i in range(count):
+                buf[(start + i) * PAGE : (start + i + 1) * PAGE, :] = bank[pages[request, first + stride * i]]
 
     collect(kbank, kbuf)
     load_v.wait()
-    load_w.start()
     collect(vbank, vbuf)
 
     def over(first, count):
@@ -327,21 +322,24 @@
         for half in range(2):
             mid = here[1 - half]
             made = []
-            for by in (1, side - 1) + ((2,) if item < 2 else ()):
+            for by in (1, side - 1):
                 got = line(item, half, lax.rem(mid + side - by, side))
                 made.append((line(item, half, mid), got, hop(1 - half, by)))
             out += moves(item, half, 3, made)
         return out
 
-    def third_phase(item):
+    def last_phase(item):
         out = []
         for half in range(2):
             mid = here[1 - half]
+            opposite = lax.rem(mid + 2, side)
             made = []
-            for by, some in ((1, pl.ds(0, side // 2)), (side - 1, pl.ds(side // 2, side // 2))):
-                sent = line(item, half, lax.rem(mid + side - by, side), some)
-                got = line(item, half, lax.rem(mid + 2, side), some)
-                made.append((sent, got, hop(1 - half, by)))
+            if item in ROUTED:
+                made.append((line(item, half, mid), line(item, half, opposite), hop(1 - half, 2)))
+            else:
+                for by, some in ((1, pl.ds(0, side // 2)), (side - 1, pl.ds(side // 2, side // 2))):
+                    sent = line(item, half, lax.rem(mid + side - by, side), some)
+                    made.append((sent, line(item, half, opposite, some), hop(1 - half, by)))
             out += moves(item, half, 5, made)
         return out
 
@@ -352,10 +350,10 @@
             copy().start()
 
     def one_two(item):
-        follow(first_phase(item), second_phase(item))
+        follow(first_phase(item), second_phase(item) + (last_phase(item) if item in ROUTED else []))
 
     def two_three(item):
-        follow(second_phase(item), third_phase(item))
+        follow(second_phase(item), [] if item in ROUTED else last_phase(item))
 
     def publish(item, rows):
         rows = rows.astype(BF16)
@@ -390,6 +388,8 @@
 
         publish(h, hidden - block_mean)
 
+    group = (DRAFTS + 1) * TREE
+
     def normalise(h):
         @pl.loop(1, ntp)
         def _(p):
@@ -397,7 +397,7 @@
             stat = stat_got.at[h, s]
             to(stat, stat, stat_ssem.at[h, s], stat_rsem.at[h, s], (g, s)).wait_recv()
 
-        follow(second_phase(h), ())
+        follow(second_phase(h) + last_phase(h), ())
 
         stats = stat_got[h].reshape(128, 128).T[0:TREE]
         mean = jnp.sum(jnp.where(lane % 8 == 0, stats, 0.0), axis=1, keepdims=True) * (1.0 / D)
@@ -407,14 +407,14 @@
             shift = stats[:, 8 * s + 2 : 8 * s + 3] - mean
             gains = jnp.concatenate([stat_got[h, s, 4:5, :], stat_got[h, s, 5:6, :]], axis=1)
             rows = jnp.concatenate([spread[h, half, s // side, s % side] for half in range(2)], axis=1)
-            normed[h * TREE : (h + 1) * TREE, s * width : (s + 1) * width] = (
+            acts[h * group : h * group + TREE, s * width : (s + 1) * width] = (
                 (rows.astype(F32) + shift) * scale * gains
             ).astype(BF16)
 
     def draft(h, k):
-        rows = slice(h * TREE, (h + 1) * TREE)
-        update = dot(normed[rows, :], dw[k])
-        own_rows = normed[rows, cols(me)].astype(F32)
+        rows = slice(h * group, h * group + TREE)
+        update = dot(acts[rows, :], dw[k])
+        own_rows = acts[rows, cols(me)].astype(F32)
         publish(2 + 2 * k + h, own_rows + update / (1.0 + jnp.exp(-update)))
 
     def item(h, k):
@@ -423,103 +423,71 @@
     share_rows(0)
     one_two(0)
     share_rows(1)
+    one_two(1)
     normalise(0)
     load_d.wait()
-    draft(0, 0)
-    one_two(1)
-    draft(0, 1)
-    draft(0, 2)
+    for k in range(DRAFTS):
+        draft(0, k)
     one_two(item(0, 0))
     normalise(1)
     draft(1, 0)
     one_two(item(0, 1))
     draft(1, 1)
+    draft(1, 2)
     one_two(item(0, 2))
     two_three(item(0, 0))
-    draft(1, 2)
+
+    square[...] = jnp.zeros_like(square)
+    square[0:4, 0:tokens] = targets[...].astype(F32)
+    wanted = square[...].T[0:tokens]
+
     one_two(item(1, 0))
     two_three(item(0, 1))
+    one_two(item(1, 1))
+    two_three(item(0, 2))
+    one_two(item(1, 2))
 
     load_w.wait()
     step = 256
     whole = vocab // step
-
-    tiles = [(i * step, step) for i in range(whole)]
-    if vocab > whole * step:
-        tiles.append((whole * step, vocab - whole * step))
-
-    def base_logits(i):
-        at, n = tiles[i]
-        logits[0:tokens, at : at + n] = dot_nt(normed[...], vw[at : at + n, :])
-
-    events = (
-        ((one_two, 1, 1), (two_three, 0, 2)),
-        ((one_two, 1, 2),),
-        ((two_three, 1, 0),),
-        (),
-        ((two_three, 1, 1),),
-        (),
-        ((two_three, 1, 2),),
-    )
-    for i in range(max(len(tiles), len(events))):
-        if i < len(tiles):
-            base_logits(i)
-        if i < len(events):
-            for event, h, k in events[i]:
-                event(item(h, k))
-
-    square[...] = jnp.zeros_like(square)
-    square[0:4, 0:tokens] = targets[...].astype(F32)
-    wanted = square[...].T[0:tokens]
-
-    drafts = DRAFTS * tokens
-
-    def some_drafts(at, n, lines):
-        total = jnp.zeros((drafts, n), F32)
-        for half in range(2):
-            for by in lines:
-                mid = lax.rem(here[1 - half] + by, side)
-                for first in range(0, side, 2):
-                    rows, weights = [], []
-                    for other in (first, first + 1):
-                        x, z = (other, mid) if half == 0 else (mid, other)
-                        rows.append(spread[2 : 2 * (DRAFTS + 1), half, x, z].reshape(drafts, half_width))
-                        place = (x * side + z) * width + half * half_width
-                        weights.append(vw[pl.ds(at, n), pl.ds(pl.multiple_of(place, half_width), half_width)])
-                    total += dot_nt(jnp.concatenate(rows, axis=1), jnp.concatenate(weights, axis=1))
-        return total
-
-    def each_tile(body):
+    entry = (lax.broadcasted_iota(jnp.int32, (1, vocab), 1) + me * vocab).astype(F32)
+
+    def vocabulary(h):
+        for k in range(DRAFTS):
+            if item(h, k) in ROUTED:
+                follow(second_phase(item(h, k)), ())
+            follow(last_phase(item(h, k)), ())
+            at = h * group + (k + 1) * TREE
+            for s in range(ntp):
+                acts[at : at + TREE, s * width : (s + 1) * width] = jnp.concatenate(
+                    [spread[item(h, k), half, s // side, s % side] for half in range(2)], axis=1
+                )
+
+        def block(at, n):
+            logits[h * group : (h + 1) * group, pl.ds(at, n)] = dot_nt(
+                acts[h * group : (h + 1) * group, :], vw[pl.ds(at, n), :]
+            )
+
         @pl.loop(0, whole)
         def _(i):
-            body(pl.multiple_of(i * step, step), step)
+            block(pl.multiple_of(i * step, step), step)
 
         if vocab > whole * step:
-            body(whole * step, vocab - whole * step)
-
-    def near(at, n):
-        logits[tokens : tokens + drafts, pl.ds(at, n)] = some_drafts(at, n, (0, 1, side - 1))
-
-    def far(at, n):
-        logits[tokens : tokens + drafts, pl.ds(at, n)] += some_drafts(at, n, (2,))
-
-    each_tile(near)
-    for k in range(DRAFTS):
-        for h in range(2):
-            follow(third_phase(item(h, k)), ())
-    each_tile(far)
-
-    entry = (lax.broadcasted_iota(jnp.int32, (1, vocab), 1) + me * vocab).astype(F32)
-    summary = jnp.zeros((tokens, 128), F32)
-    lane = lax.broadcasted_iota(jnp.int32, (tokens, 128), 1)
-    for k in range(DRAFTS + 1):
-        x = logits[k * tokens : (k + 1) * tokens, :]
-        top = jnp.max(x, axis=1, keepdims=True)
-        total = jnp.sum(jnp.exp(x - top), axis=1, keepdims=True)
-        picked = jnp.sum(jnp.where(entry == wanted[:, k : k + 1], x, 0.0), axis=1, keepdims=True)
-        for c, value in enumerate((top, total, picked)):
-            summary = jnp.where(lane == 8 * c + k, value, summary)
-    square[0:tokens, :] = summary
+            block(whole * step, vocab - whole * step)
+
+        summary = jnp.zeros((TREE, 128), F32)
+        for k in range(DRAFTS + 1):
+            x = logits[h * group + k * TREE : h * group + (k + 1) * TREE, :]
+            top = jnp.max(x, axis=1, keepdims=True)
+            total = jnp.sum(jnp.exp(x - top), axis=1, keepdims=True)
+            target = wanted[h * TREE : (h + 1) * TREE, k : k + 1]
+            picked = jnp.sum(jnp.where(entry == target, x, 0.0), axis=1, keepdims=True)
+            for c, value in enumerate((top, total, picked)):
+                summary = jnp.where(lane == 8 * c + k, value, summary)
+        square[h * TREE : (h + 1) * TREE, :] = summary
+
+    vocabulary(0)
+    vocabulary(1)
     fin_got[me] = square[...].T[0:24]
 
     @pl.loop(1, ntp)
@@ -528,7 +496,7 @@
         to(fin_got.at[me], fin_got.at[me], fin_ssem.at[t], fin_rsem.at[me], (g, t)).start()
 
     for i in range(2 * (DRAFTS + 1)):
-        for copy, _ in first_phase(i) + second_phase(i) + (third_phase(i) if i >= 2 else []):
+        for copy, _ in first_phase(i) + second_phase(i) + last_phase(i):
             copy().wait_send()
     ask.wait_send()
     give_o.wait_send()
@@ -606,7 +574,7 @@
             pltpu.VMEM((2, ntp, TREE, width), BF16),
             pltpu.VMEM((2, ntp, TREE, width), BF16),
             pltpu.VMEM((2, ntp, 8, 128), F32),
-            pltpu.VMEM((tokens, D), BF16),
+            pltpu.VMEM(((DRAFTS + 1) * tokens, D), BF16),
             pltpu.VMEM((2 * (DRAFTS + 1), 2, side, side, TREE, width // 2), BF16),
             pltpu.VMEM(((DRAFTS + 1) * tokens, vocab_weight.shape[0]), F32),
             pltpu.VMEM((ntp, 24, 128), F32),

time: 68.2 us -> 70.4 us (1.032)
  Pallas kernels: 64.9 us -> 67 us
    pallas_call x1, Pallas kernels: 64.9 us -> 67 us  [shards(): pl.pallas_call(functools.partial(kernel, ntp), out_shape=(jax.ShapeDtypeS...]
where the time goes in v5:
time: 70.4 us; the launch traced here: 70.2 us
  Pallas kernels  67 us (95%)
  local copies, waits for them, and re-layouts  2.53 us (4%)
    pallas_call x1, Pallas kernels, shards(): pl.pallas_call(functools.partial(kernel, ntp), out_shape=(jax.ShapeDtypeS...  67 us
    unnamed x2, local copies, waits for them, and re-layouts  2.53 us

profile of v5, /device:TPU:0, one launch (start us, length us, event | category | flops | bytes accessed | tf_op | source)
XLA Modules:
  0.0 70.2 jit_solution(16565477929438076454)
XLA Ops:
  0.6 67.0 %shard_map.131 = (f32[4,96]{1,0:T(4,128)}, bf16[2,8,256]{2,1,0:T(8,128)(2,1)}) custom-call(bf16[96,256]{1,0:T(8,128)(2,1)} %residual.1, bf16[3,96,256]{2,1,0:T(8,128)(2,1)} %tree.1, bf16[2,32,128,256]{3,2,1,0:T(8,128)(2,1)} %pool.1, s32[16,28]{1,0:T(8,128)} %pages.1, s32[16]{0:T(128)} %lens.1, s32[16,48]{1,0:T(8,128)} %parents.1, s32[2,4]{1,0:T(2,128)} %accepted.1, ...), custom_call_target="tpu_custom_call" | custom-call | flops 6200000000 | bytes 27000000 | tf_op jit(solution)/shard_map/pallas_call | solution.py:553
  67.7 1.2 %copy.16 = f32[4,96]{1,0:T(4,128)} copy(f32[4,96]{1,0:T(4,128)} %get-tuple-element.4) | data formatting | bytes 3072
  68.9 1.3 %copy.17 = bf16[2,8,256]{2,1,0:T(8,128)(2,1)} copy(bf16[2,8,256]{2,1,0:T(8,128)(2,1)} %get-tuple-element.5) | data formatting | bytes 16384

commit v6 on v5

--- a/solution.py
+++ b/solution.py
@@ -17,6 +17,7 @@
 PAGE = 128
 DRAFTS = 3
 EPSILON = 1e-05
+STEP = 512
 ROUTED = (0, 1, 3, 5, 7)
 F32 = jnp.float32
 BF16 = jnp.bfloat16
@@ -388,8 +389,6 @@
 
         publish(h, hidden - block_mean)
 
-    group = (DRAFTS + 1) * TREE
-
     def normalise(h):
         @pl.loop(1, ntp)
         def _(p):
@@ -407,12 +406,12 @@
             shift = stats[:, 8 * s + 2 : 8 * s + 3] - mean
             gains = jnp.concatenate([stat_got[h, s, 4:5, :], stat_got[h, s, 5:6, :]], axis=1)
             rows = jnp.concatenate([spread[h, half, s // side, s % side] for half in range(2)], axis=1)
-            acts[h * group : h * group + TREE, s * width : (s + 1) * width] = (
+            acts[h * TREE : (h + 1) * TREE, s * width : (s + 1) * width] = (
                 (rows.astype(F32) + shift) * scale * gains
             ).astype(BF16)
 
     def draft(h, k):
-        rows = slice(h * group, h * group + TREE)
+        rows = slice(h * TREE, (h + 1) * TREE)
         update = dot(acts[rows, :], dw[k])
         own_rows = acts[rows, cols(me)].astype(F32)
         publish(2 + 2 * k + h, own_rows + update / (1.0 + jnp.exp(-update)))
@@ -441,53 +440,58 @@
     square[0:4, 0:tokens] = targets[...].astype(F32)
     wanted = square[...].T[0:tokens]
 
+    load_w.wait()
+    entry = (lax.broadcasted_iota(jnp.int32, (1, vocab), 1) + me * vocab).astype(F32)
+    lane = lax.broadcasted_iota(jnp.int32, (tokens, 128), 1)
+
+    def block(first, rows, at, n):
+        logits[first : first + rows, pl.ds(at, n)] = dot_nt(acts[first : first + rows, :], vw[pl.ds(at, n), :])
+
+    def tally(k, summary):
+        x = logits[k * tokens : (k + 1) * tokens, :]
+        top = jnp.max(x, axis=1, keepdims=True)
+        total = jnp.sum(jnp.exp(x - top), axis=1, keepdims=True)
+        picked = jnp.sum(jnp.where(entry == wanted[:, k : k + 1], x, 0.0), axis=1, keepdims=True)
+        for c, value in enumerate((top, total, picked)):
+            summary = jnp.where(lane == 8 * c + k, value, summary)
+        return summary
+
+    def base(first, last):
+        step = 256
+        for at in range(first * step, min(last * step, vocab), step):
+            block(0, tokens, at, min(step, vocab - at))
+
     one_two(item(1, 0))
     two_three(item(0, 1))
     one_two(item(1, 1))
+    base(0, 2)
     two_three(item(0, 2))
     one_two(item(1, 2))
-
-    load_w.wait()
-    step = 256
-    whole = vocab // step
-    entry = (lax.broadcasted_iota(jnp.int32, (1, vocab), 1) + me * vocab).astype(F32)
-
-    def vocabulary(h):
-        for k in range(DRAFTS):
-            if item(h, k) in ROUTED:
-                follow(second_phase(item(h, k)), ())
-            follow(last_phase(item(h, k)), ())
-            at = h * group + (k + 1) * TREE
+    base(2, 8)
+    summary = tally(0, jnp.zeros((tokens, 128), F32))
+
+    for k in range(DRAFTS):
+        for h in range(2):
+            i = item(h, k)
+            follow((second_phase(i) if i in ROUTED else []) + last_phase(i), ())
+            at = (2 * (k + 1) + h) * TREE
             for s in range(ntp):
                 acts[at : at + TREE, s * width : (s + 1) * width] = jnp.concatenate(
-                    [spread[item(h, k), half, s // side, s % side] for half in range(2)], axis=1
+                    [spread[i, half, s // side, s % side] for half in range(2)], axis=1
                 )
 
-        def block(at, n):
-            logits[h * group : (h + 1) * group, pl.ds(at, n)] = dot_nt(
-                acts[h * group : (h + 1) * group, :], vw[pl.ds(at, n), :]
-            )
-
-        @pl.loop(0, whole)
-        def _(i):
-            block(pl.multiple_of(i * step, step), step)
-
-        if vocab > whole * step:
-            block(whole * step, vocab - whole * step)
-
-        summary = jnp.zeros((TREE, 128), F32)
-        for k in range(DRAFTS + 1):
-            x = logits[h * group + k * TREE : h * group + (k + 1) * TREE, :]
-            top = jnp.max(x, axis=1, keepdims=True)
-            total = jnp.sum(jnp.exp(x - top), axis=1, keepdims=True)
-            target = wanted[h * TREE : (h + 1) * TREE, k : k + 1]
-            picked = jnp.sum(jnp.where(entry == target, x, 0.0), axis=1, keepdims=True)
-            for c, value in enumerate((top, total, picked)):
-                summary = jnp.where(lane == 8 * c + k, value, summary)
-        square[h * TREE : (h + 1) * TREE, :] = summary
-
-    vocabulary(0)
-    vocabulary(1)
+    step = STEP
+    whole = vocab // step
+
+    @pl.loop(0, whole)
+    def _(i):
+        block(tokens, DRAFTS * tokens, pl.multiple_of(i * step, step), step)
+
+    if vocab > whole * step:
+        block(tokens, DRAFTS * tokens, whole * step, vocab - whole * step)
+    for k in range(1, DRAFTS + 1):
+        summary = tally(k, summary)
+    square[0:tokens, :] = summary
     fin_got[me] = square[...].T[0:24]
 
     @pl.loop(1, ntp)

time: 70.4 us -> 65 us (0.923)
  Pallas kernels: 67 us -> 61.6 us
    pallas_call x1, Pallas kernels: 67 us -> 61.6 us  [shards(): pl.pallas_call(functools.partial(kernel, ntp), out_shape=(jax.ShapeDtypeS...]
where the time goes in v6:
time: 65 us; the launch traced here: 64.8 us
  Pallas kernels  61.6 us (95%)
  local copies, waits for them, and re-layouts  2.53 us (4%)
    pallas_call x1, Pallas kernels, shards(): pl.pallas_call(functools.partial(kernel, ntp), out_shape=(jax.ShapeDtypeS...  61.6 us
    unnamed x2, local copies, waits for them, and re-layouts  2.53 us

profile of v6, /device:TPU:0, one launch (start us, length us, event | category | flops | bytes accessed | tf_op | source)
XLA Modules:
  0.0 64.8 jit_solution(11820635254623019335)
XLA Ops:
  0.6 61.6 %shard_map.131 = (f32[4,96]{1,0:T(4,128)}, bf16[2,8,256]{2,1,0:T(8,128)(2,1)}) custom-call(bf16[96,256]{1,0:T(8,128)(2,1)} %residual.1, bf16[3,96,256]{2,1,0:T(8,128)(2,1)} %tree.1, bf16[2,32,128,256]{3,2,1,0:T(8,128)(2,1)} %pool.1, s32[16,28]{1,0:T(8,128)} %pages.1, s32[16]{0:T(128)} %lens.1, s32[16,48]{1,0:T(8,128)} %parents.1, s32[2,4]{1,0:T(2,128)} %accepted.1, ...), custom_call_target="tpu_custom_call" | custom-call | flops 6200000000 | bytes 27000000 | tf_op jit(solution)/shard_map/pallas_call | solution.py:557
  62.3 1.2 %copy.16 = f32[4,96]{1,0:T(4,128)} copy(f32[4,96]{1,0:T(4,128)} %get-tuple-element.4) | data formatting | bytes 3072
  63.5 1.3 %copy.17 = bf16[2,8,256]{2,1,0:T(8,128)(2,1)} copy(bf16[2,8,256]{2,1,0:T(8,128)(2,1)} %get-tuple-element.5) | data formatting | bytes 16384

commit v7 on v6

--- a/solution.py
+++ b/solution.py
@@ -61,14 +61,16 @@
 
 def cache_part(queries, keys, values, slopes, length, first, stride):
     span = keys.shape[0]
-    scores = dot_nt(queries, keys) * (1.0 / math.sqrt(HD))
+    rows = queries.shape[0] // 2
     index = lax.broadcasted_iota(jnp.int32, (1, span), 1)
     place = ((index >> 7) * stride + first) * PAGE + (index & (PAGE - 1))
     relative = place.astype(F32) - length
     exists = relative < 0.0
-    scores = jnp.where(exists, scores + slopes * relative, -1e30)
-    top = jnp.max(scores, axis=1, keepdims=True)
-    weights = jnp.where(exists, jnp.exp(scores - top), 0.0)
+    bias = [jnp.where(exists, slopes[h * rows : h * rows + 1] * relative, -1e30) for h in range(2)]
+    scores = dot_nt(queries, keys) * (1.0 / math.sqrt(HD))
+    scores = jnp.concatenate([scores[:rows] + bias[0], scores[rows:] + bias[1]], axis=0)
+    top = jnp.maximum(jnp.max(scores, axis=1, keepdims=True), -1e29)
+    weights = jnp.exp(scores - top)
     total = jnp.sum(weights, axis=1, keepdims=True)
     return top, total, own_heads(dot(weights.astype(BF16), values))
 
@@ -202,19 +204,13 @@
 
     load_k.wait()
 
-    def collect(bank, buf):
-        for start, count, request, first, stride in (
-            (0, HALF, guest, 1, 2),
-            (HALF, HALF, mine, 0, 2),
-            (2 * HALF, SHORT_PAGES, 2 * g, 0, 1),
-        ):
-
-            for i in range(count):
-                buf[(start + i) * PAGE : (start + i + 1) * PAGE, :] = bank[pages[request, first + stride * i]]
-
-    collect(kbank, kbuf)
+    def collect(bank, buf, start, count, request, first, stride):
+        for i in range(count):
+            buf[(start + i) * PAGE : (start + i + 1) * PAGE, :] = bank[pages[request, first + stride * i]]
+
     load_v.wait()
-    collect(vbank, vbuf)
+    for bank, buf in ((kbank, kbuf), (vbank, vbuf)):
+        collect(bank, buf, 2 * HALF, SHORT_PAGES, 2 * g, 0, 1)
 
     def over(first, count):
         return pl.ds(first * PAGE, count * PAGE)
@@ -258,6 +254,9 @@
     load_o.wait()
     project(0, join(of_request(0), short_part))
     long = of_request(1)
+    for bank, buf in ((kbank, kbuf), (vbank, vbuf)):
+        collect(bank, buf, 0, HALF, guest, 1, 2)
+        collect(bank, buf, HALF, HALF, mine, 0, 2)
 
     ask.wait_recv()
     top, total, out = cache_part(
@@ -464,10 +463,10 @@
     one_two(item(1, 0))
     two_three(item(0, 1))
     one_two(item(1, 1))
-    base(0, 2)
+    one_two(item(1, 2))
+    base(0, 1)
     two_three(item(0, 2))
-    one_two(item(1, 2))
-    base(2, 8)
+    base(1, 8)
     summary = tally(0, jnp.zeros((tokens, 128), F32))
 
     for k in range(DRAFTS):

time: 65 us -> 64.7 us (level)
  no operation moved by 1% of the time
where the time goes in v7:
time: 64.7 us; the launch traced here: 64.5 us
  Pallas kernels  61.4 us (95%)
  local copies, waits for them, and re-layouts  2.53 us (4%)
    pallas_call x1, Pallas kernels, shards(): pl.pallas_call(functools.partial(kernel, ntp), out_shape=(jax.ShapeDtypeS...  61.4 us
    unnamed x2, local copies, waits for them, and re-layouts  2.53 us

profile of v7, /device:TPU:0, one launch (start us, length us, event | category | flops | bytes accessed | tf_op | source)
XLA Modules:
  0.0 64.5 jit_solution(4040587214587345621)
XLA Ops:
  0.6 61.4 %shard_map.131 = (f32[4,96]{1,0:T(4,128)}, bf16[2,8,256]{2,1,0:T(8,128)(2,1)}) custom-call(bf16[96,256]{1,0:T(8,128)(2,1)} %residual.1, bf16[3,96,256]{2,1,0:T(8,128)(2,1)} %tree.1, bf16[2,32,128,256]{3,2,1,0:T(8,128)(2,1)} %pool.1, s32[16,28]{1,0:T(8,128)} %pages.1, s32[16]{0:T(128)} %lens.1, s32[16,48]{1,0:T(8,128)} %parents.1, s32[2,4]{1,0:T(2,128)} %accepted.1, ...), custom_call_target="tpu_custom_call" | custom-call | flops 6200000000 | bytes 27000000 | tf_op jit(solution)/shard_map/pallas_call | solution.py:556
  62.0 1.2 %copy.16 = f32[4,96]{1,0:T(4,128)} copy(f32[4,96]{1,0:T(4,128)} %get-tuple-element.4) | data formatting | bytes 3072
  63.2 1.3 %copy.17 = bf16[2,8,256]{2,1,0:T(8,128)(2,1)} copy(bf16[2,8,256]{2,1,0:T(8,128)(2,1)} %get-tuple-element.5) | data formatting | bytes 16384

commit v8 on v7

--- a/solution.py
+++ b/solution.py
@@ -18,7 +18,7 @@
 DRAFTS = 3
 EPSILON = 1e-05
 STEP = 512
-ROUTED = (0, 1, 3, 5, 7)
+ROUTED = (0, 1, 5, 7)
 F32 = jnp.float32
 BF16 = jnp.bfloat16
 MESH = pl.DeviceIdType.MESH
@@ -466,7 +466,9 @@
     one_two(item(1, 2))
     base(0, 1)
     two_three(item(0, 2))
-    base(1, 8)
+    base(1, 2)
+    two_three(item(1, 0))
+    base(2, 8)
     summary = tally(0, jnp.zeros((tokens, 128), F32))
 
     for k in range(DRAFTS):

time: 64.7 us -> 64.8 us (level)
  no operation moved by 1% of the time
where the time goes in v8:
time: 64.8 us; the launch traced here: 64.6 us
  Pallas kernels  61.4 us (95%)
  local copies, waits for them, and re-layouts  2.53 us (4%)
    pallas_call x1, Pallas kernels, shards(): pl.pallas_call(functools.partial(kernel, ntp), out_shape=(jax.ShapeDtypeS...  61.4 us
    unnamed x2, local copies, waits for them, and re-layouts  2.53 us

profile of v8, /device:TPU:0, one launch (start us, length us, event | category | flops | bytes accessed | tf_op | source)
XLA Modules:
  0.0 64.6 jit_solution(14143486362881397709)
XLA Ops:
  0.6 61.4 %shard_map.131 = (f32[4,96]{1,0:T(4,128)}, bf16[2,8,256]{2,1,0:T(8,128)(2,1)}) custom-call(bf16[96,256]{1,0:T(8,128)(2,1)} %residual.1, bf16[3,96,256]{2,1,0:T(8,128)(2,1)} %tree.1, bf16[2,32,128,256]{3,2,1,0:T(8,128)(2,1)} %pool.1, s32[16,28]{1,0:T(8,128)} %pages.1, s32[16]{0:T(128)} %lens.1, s32[16,48]{1,0:T(8,128)} %parents.1, s32[2,4]{1,0:T(2,128)} %accepted.1, ...), custom_call_target="tpu_custom_call" | custom-call | flops 6200000000 | bytes 27000000 | tf_op jit(solution)/shard_map/pallas_call | solution.py:558
  62.1 1.2 %copy.16 = f32[4,96]{1,0:T(4,128)} copy(f32[4,96]{1,0:T(4,128)} %get-tuple-element.4) | data formatting | bytes 3072
  63.3 1.3 %copy.17 = bf16[2,8,256]{2,1,0:T(8,128)(2,1)} copy(bf16[2,8,256]{2,1,0:T(8,128)(2,1)} %get-tuple-element.5) | data formatting | bytes 16384
